TPU v7x, 32 devices: a whole 2x2x4 slice. The times are simulated.
32 devices in a mesh: dp: 2 (over x), lat: 4 (over y, core), lon: 4 (over z).
Axes of the slice: x: 2, y: 2, z: 4, core: 2. Of those that a mesh axis runs over, the one named last changes fastest.
Arguments:
- inputs: bfloat16 [2, 128, 64, 1024], P('dp', 'lat', 'lon'), may hold values from -40 to 40
- grad_out: bfloat16 [2, 128, 64, 1024], P('dp', 'lat', 'lon'), may hold values from -6 to 6
- w_qkv: bfloat16 [1024, 3072], replicated, may hold values from -0.1875 to 0.1875
Outputs:
- grad_inputs: bfloat16 [2, 128, 64, 1024], P('dp', 'lat', 'lon')
- grad_w_qkv: float32 [1024, 3072], P(('dp', 'lat', 'lon'))
All inputs are finite; a program needn't handle non-finite values.
Results may differ from a plain program's by a relative error of at most 0.011.
Values may be sent and summed in bfloat16 or wider, within the bound.
No kernel may reach another device: no remote copies, remote signals or barrier semaphores. Data moves between devices by JAX's collectives and lax.ppermute only.
A program may use at most 192 MiB of HBM per device.

v0:
```python
import functools

import jax
import jax.numpy as jnp
import numpy as np
from jax import lax
from jax.experimental import pallas as pl
from jax.experimental.pallas import tpu as pltpu
from jax.sharding import PartitionSpec as P

HEADS = 16
WIN = 13
MARGIN = WIN // 2
TILE_R = 4
GROUP = 4
KEY_COLS = 32
HALO_COLS = 16
REGION_R = 16
PAD_R = 2
EDGE_R = MARGIN + PAD_R
NEG = -1e30
BF = jnp.bfloat16
F32 = jnp.float32
MIB = 1024 * 1024
FINISH_FLOPS = 6 * 10**9
LANES = 128

NT = (((1,), (1,)), ((), ()))
TN = (((0,), (0,)), ((), ()))
NN = (((1,), (0,)), ((), ()))


def dot(a, b, dims=NN):
    return lax.dot_general(a, b, dims, preferred_element_type=F32)


def region_top(tile, band_start, band_rows, total_rows):
    lowest = jnp.where(band_start == 0, TILE_R, 0)
    highest = jnp.where(band_start + band_rows == total_rows, band_rows - 2 * TILE_R, band_rows)
    return jnp.clip(tile * TILE_R, lowest, highest)


def mask_kernel(band_rows, band_cols, total_rows, start_ref, mask_ref):
    band_start = start_ref[0]
    tile = pl.program_id(0)
    shape = mask_ref.shape[1:]
    first = region_top(tile, band_start, band_rows, total_rows)
    key = lax.broadcasted_iota(jnp.int32, shape, 0)
    query = lax.broadcasted_iota(jnp.int32, shape, 1) % (TILE_R * band_cols)
    key_row = band_start - MARGIN + first + key // KEY_COLS
    place = key % KEY_COLS
    query_row = band_start + tile * TILE_R + query // band_cols
    query_col = query % band_cols
    window = jnp.clip(query_row - MARGIN, 0, total_rows - WIN)
    row_inside = (key_row >= window) & (key_row < window + WIN)
    key_col = jnp.where(
        place < band_cols,
        place,
        jnp.where(place < band_cols + MARGIN, place - band_cols - MARGIN, place - MARGIN),
    )
    col_inside = (jnp.abs(key_col - query_col) <= MARGIN) & (place < band_cols + 2 * MARGIN)
    mask_ref[0] = jnp.where(row_inside & col_inside, 0.0, NEG).astype(BF)


def window_masks(start, band_rows, band_cols, total_rows):
    tiles = band_rows // TILE_R
    shape = (REGION_R * KEY_COLS, 2 * TILE_R * band_cols)
    return pl.pallas_call(
        functools.partial(mask_kernel, band_rows, band_cols, total_rows),
        grid=(tiles,),
        in_specs=[pl.BlockSpec(memory_space=pltpu.SMEM)],
        out_specs=pl.BlockSpec((1,) + shape, lambda t: (t, 0, 0)),
        out_shape=jax.ShapeDtypeStruct((tiles,) + shape, BF),
        cost_estimate=pl.CostEstimate(flops=10**7, bytes_accessed=2**21, transcendentals=0),
    )(start)


def attention_kernel(band_rows, band_cols, total_rows, head_width, extra, first, count, *refs):
    (start_ref, mask_ref, left_ref, right_ref, above_ref, below_ref, cl_ref, cr_ref,
     qkv_hbm, grad_hbm, w_hbm) = refs[:11]
    (dq_ref, top_ref, bottom_ref, mid_ref, to_left_ref, to_right_ref,
     halo_ref, spot_ref, q_ref, k_ref, v_ref, dk_ref, dv_ref,
     own_refs, w_refs, own_sem, w_sem) = refs[11 + extra :]
    band_start = start_ref[0]
    tiles = band_rows // TILE_R
    queries = TILE_R * band_cols
    keys = REGION_R * KEY_COLS
    width = GROUP * head_width
    lanes = GROUP * queries
    region_rows = band_rows + 2 * MARGIN
    side = MARGIN * band_rows
    edge = MARGIN * band_cols
    corner = 2 * MARGIN * EDGE_R
    at_above = 2 * side
    at_below = at_above + edge
    at_cl = at_below + edge
    at_cr = at_cl + corner
    halves = [(i, slice(i * LANES, (i + 1) * LANES)) for i in range(width // LANES)]

    step = pl.program_id(0)
    groups = HEADS // GROUP

    def copies(slot):
        at = lambda part: pl.ds((part * groups + first + slot) * width, width)
        own = [
            pltpu.make_async_copy(source.at[:, at(part)], own_refs.at[slot, i], own_sem.at[slot, i])
            for i, (source, part) in enumerate(
                ((qkv_hbm, 0), (qkv_hbm, 1), (qkv_hbm, 2), (grad_hbm, 0))
            )
        ]
        weights = [
            pltpu.make_async_copy(w_hbm.at[:, at(1 + i)], w_refs.at[slot, i], w_sem.at[slot, i])
            for i in range(2)
        ]
        return weights + own

    @pl.when(step == 0)
    def _():
        for slot in range(count):
            for copy in copies(slot):
                copy.start()
        halo_ref[:side] = left_ref[...]
        halo_ref[side:at_above] = right_ref[...]
        halo_ref[at_above:at_below] = above_ref[...]
        halo_ref[at_below:at_cl] = below_ref[...]
        halo_ref[at_cl : at_cl + corner] = cl_ref[...]
        halo_ref[at_cr : at_cr + corner] = cr_ref[...]
        spot_ref[...] = jnp.zeros_like(spot_ref)

    def place(target, own, weights):
        fresh = dot(halo_ref[...], weights)
        for col in range(MARGIN):
            start = MARGIN * HALO_COLS + col
            for part, at in halves:
                spot_ref[part, pl.ds(start, band_rows, stride=HALO_COLS), :] = fresh[
                    col * band_rows : (col + 1) * band_rows, at
                ]
                spot_ref[part, pl.ds(start + MARGIN, band_rows, stride=HALO_COLS), :] = fresh[
                    side + col * band_rows : side + (col + 1) * band_rows, at
                ]
        for corner_at, offset in ((at_cl, 0), (at_cr, MARGIN)):
            for rim in range(2):
                first = rim * (MARGIN + band_rows) * HALO_COLS + offset
                for col in range(MARGIN):
                    base = corner_at + (rim * MARGIN + col) * EDGE_R
                    for part, at in halves:
                        spot_ref[part, pl.ds(first + col, MARGIN, stride=HALO_COLS), :] = fresh[
                            base : base + MARGIN, at
                        ]
        for row in range(region_rows):
            base = row * KEY_COLS
            inner = row - MARGIN
            if inner < 0:
                ours = fresh[at_above + row * band_cols : at_above + (row + 1) * band_cols].astype(BF)
            elif inner < band_rows:
                ours = own[inner * band_cols : (inner + 1) * band_cols, :]
            else:
                past = at_below + (inner - band_rows) * band_cols
                ours = fresh[past : past + band_cols].astype(BF)
            target[base : base + band_cols, :] = ours
            for part, at in halves:
                target[base + band_cols : base + KEY_COLS, at] = spot_ref[
                    part, row * HALO_COLS : (row + 1) * HALO_COLS, :
                ].astype(BF)

    for slot in range(count):

        @pl.when(step == slot)
        def _():
            for copy in copies(slot):
                copy.wait()

    grad_ref = own_refs.at[step, 3]
    place(k_ref, own_refs.at[step, 1], w_refs[step, 0])
    place(v_ref, own_refs.at[step, 2], w_refs[step, 1])
    q_ref[...] = own_refs[step, 0] * BF(head_width**-0.5)
    dk_ref[...] = jnp.zeros_like(dk_ref)
    dv_ref[...] = jnp.zeros_like(dv_ref)

    def spread(rows):
        block = jnp.concatenate([rows] * GROUP, axis=0)
        head_row = lax.broadcasted_iota(jnp.int32, (lanes, width), 0) // queries
        head_col = lax.broadcasted_iota(jnp.int32, (lanes, width), 1) // head_width
        return jnp.where(head_row == head_col, block, jnp.zeros_like(block))

    def one_tile(tile, carry):
        first = region_top(tile, band_start, band_rows, total_rows)
        region = pl.ds(pl.multiple_of(first * KEY_COLS, TILE_R * KEY_COLS), keys)
        total = pl.ds(pl.multiple_of((first + PAD_R) * KEY_COLS, PAD_R * KEY_COLS), keys)
        mine = pl.ds(pl.multiple_of(tile * queries, queries), queries)
        q_wide = spread(q_ref[mine, :])
        g_wide = spread(grad_ref[mine, :])
        mask = mask_ref[tile].astype(F32)
        scores = dot(k_ref[region, :], q_wide, NT) + jnp.concatenate([mask, mask], axis=1)
        dots = dot(v_ref[region, :], g_wide, NT)
        exponent = jnp.exp(scores - jnp.max(scores, axis=0, keepdims=True))
        inverse = 1.0 / jnp.sum(exponent, axis=0, keepdims=True)
        delta = jnp.sum(exponent * dots, axis=0, keepdims=True) * inverse
        attn = exponent * inverse
        dscore = (attn * (dots - delta)).astype(BF)
        dv = dot(attn.astype(BF), g_wide)
        dk = dot(dscore, q_wide)
        for part, at in halves:
            dv_ref[part, total, :] += dv[:, at]
            dk_ref[part, total, :] += dk[:, at]
        dq_wide = dot(dscore, k_ref[region, :], TN)
        head_col = lax.broadcasted_iota(jnp.int32, (queries, width), 1) // head_width
        dq = jnp.zeros((queries, width), F32)
        for head in range(GROUP):
            dq = jnp.where(head_col == head, dq_wide[head * queries : (head + 1) * queries], dq)
        dq_ref[mine, :] = (dq * head_width**-0.5).astype(BF)
        return carry

    lax.fori_loop(0, tiles, one_tile, 0, unroll=4)

    middle = (PAD_R + MARGIN) * KEY_COLS
    below = (PAD_R + MARGIN + band_rows) * KEY_COLS
    for part, acc in enumerate((dk_ref, dv_ref)):
        for lane, at in halves:
            for row in range(MARGIN):
                here = slice(row * band_cols, (row + 1) * band_cols)
                for start, out in ((PAD_R * KEY_COLS, top_ref), (below, bottom_ref)):
                    start = start + row * KEY_COLS
                    out[part, here, at] = acc[lane, start : start + band_cols, :].astype(BF)
            for pair in range(MARGIN):
                here = slice(edge + pair * 2 * EDGE_R, edge + (pair + 1) * 2 * EDGE_R)
                for start, out in ((0, top_ref), (below, bottom_ref)):
                    start = start + band_cols + 2 * pair
                    out[part, here, at] = jnp.concatenate(
                        [
                            acc[lane, pl.ds(start, EDGE_R, stride=KEY_COLS), :],
                            acc[lane, pl.ds(start + 1, EDGE_R, stride=KEY_COLS), :],
                        ],
                        axis=0,
                    ).astype(BF)
            for row in range(band_rows):
                base = middle + row * KEY_COLS
                mid_ref[part, row * band_cols : (row + 1) * band_cols, at] = acc[
                    lane, base : base + band_cols, :
                ].astype(BF)
            for col in range(MARGIN):
                here = slice(col * band_rows, (col + 1) * band_rows)
                start = middle + band_cols + col
                to_left_ref[part, here, at] = acc[
                    lane, pl.ds(start, band_rows, stride=KEY_COLS), :
                ].astype(BF)
                to_right_ref[part, here, at] = acc[
                    lane, pl.ds(start + MARGIN, band_rows, stride=KEY_COLS), :
                ].astype(BF)


def attention_grads(
    first, count, slots, start, masks, halo, qkv, grad_out, w_qkv, shape, before, after
):
    band_rows, band_cols, total_rows = shape
    tokens, width = grad_out.shape
    head_width = width // HEADS
    block = GROUP * head_width
    region_tokens = (band_rows + 2 * MARGIN) * KEY_COLS
    total_tokens = (band_rows + 2 * MARGIN + 2 * PAD_R) * KEY_COLS
    side = MARGIN * band_rows
    edge = MARGIN * (band_cols + 2 * EDGE_R)
    corner = 2 * MARGIN * EDGE_R
    halo_tokens = 2 * (side + MARGIN * band_cols + corner)
    whole = lambda g: (0, 0)
    column = lambda offset: (lambda g: (0, offset + first + g))
    slot = lambda g: (0, 0, first % slots + g)
    halves = [(2, edge), (2, edge), (2, tokens), (2, side), (2, side)]
    out_shape = [jax.ShapeDtypeStruct((tokens, width), BF)] + [
        jax.ShapeDtypeStruct(s + (slots * block,), BF) for s in halves
    ]
    aliases = {}
    if before:
        aliases = {11 + i: place for i, (place, _) in enumerate(before)}
    return pl.pallas_call(
        functools.partial(
            attention_kernel, band_rows, band_cols, total_rows, head_width,
            len(before) + len(after), first, count,
        ),
        grid=(count,),
        in_specs=[
            pl.BlockSpec(memory_space=pltpu.SMEM),
            pl.BlockSpec(masks.shape, lambda g: (0, 0, 0)),
        ]
        + [pl.BlockSpec(piece.shape, whole) for piece in halo]
        + [pl.BlockSpec(memory_space=pltpu.HBM)] * 3
        + [pl.BlockSpec(memory_space=pl.ANY)] * (len(before) + len(after)),
        out_specs=[pl.BlockSpec((tokens, block), column(0))]
        + [pl.BlockSpec(s + (block,), slot) for s in halves],
        out_shape=out_shape,
        input_output_aliases=aliases,
        scratch_shapes=[
            pltpu.VMEM((halo_tokens, width), BF),
            pltpu.VMEM((block // LANES, (band_rows + 2 * MARGIN) * HALO_COLS, LANES), F32),
            pltpu.VMEM((tokens, block), BF),
            pltpu.VMEM((region_tokens, block), BF),
            pltpu.VMEM((region_tokens, block), BF),
            pltpu.VMEM((block // LANES, total_tokens, LANES), F32),
            pltpu.VMEM((block // LANES, total_tokens, LANES), F32),
            pltpu.VMEM((count, 4, tokens, block), BF),
            pltpu.VMEM((count, 2, width, block), BF),
            pltpu.SemaphoreType.DMA((count, 4)),
            pltpu.SemaphoreType.DMA((count, 2)),
        ],
        compiler_params=pltpu.CompilerParams(
            dimension_semantics=("arbitrary",), vmem_limit_bytes=30 * MIB
        ),
        cost_estimate=pl.CostEstimate(
            flops=count * 14 * 10**9, bytes_accessed=count * 8 * MIB, transcendentals=count * 10**6
        ),
    )(start, masks, *halo, qkv, grad_out, w_qkv, *[a for _, a in before], *after)


def on_chip(kernel, out_shape, operands, after=(), scratch=(), flops=10**5):
    count = len(operands)

    def run(*refs):
        kernel(*refs[:count], *refs[count + len(after) :])

    return pl.pallas_call(
        run,
        in_specs=[pl.BlockSpec(memory_space=pltpu.VMEM)] * count
        + [pl.BlockSpec(memory_space=pl.ANY)] * len(after),
        out_specs=[pl.BlockSpec(memory_space=pltpu.VMEM)] * len(out_shape),
        out_shape=[jax.ShapeDtypeStruct(s, d) for s, d in out_shape],
        scratch_shapes=list(scratch),
        compiler_params=pltpu.CompilerParams(vmem_limit_bytes=24 * MIB),
        cost_estimate=pl.CostEstimate(flops=flops, bytes_accessed=10**4, transcendentals=0),
    )(*operands, *after)


def lanes_of(width):
    return [(i, slice(i * LANES, (i + 1) * LANES)) for i in range(width // LANES)]


def project(own, w_qkv, after):
    tokens, width = own.shape
    columns = w_qkv.shape[1]
    block = 4 * LANES

    def kernel(own_ref, w_ref, *refs):
        refs[-1][...] = dot(own_ref[...], w_ref[...]).astype(BF)

    return pl.pallas_call(
        kernel,
        grid=(columns // block,),
        in_specs=[
            pl.BlockSpec((tokens, width), lambda g: (0, 0)),
            pl.BlockSpec((width, block), lambda g: (0, g)),
        ]
        + [pl.BlockSpec(memory_space=pl.ANY)] * len(after),
        out_specs=pl.BlockSpec((tokens, block), lambda g: (0, g)),
        out_shape=jax.ShapeDtypeStruct((tokens, columns), BF),
        compiler_params=pltpu.CompilerParams(vmem_limit_bytes=24 * MIB),
        cost_estimate=pl.CostEstimate(flops=10**9, bytes_accessed=MIB, transcendentals=0),
    )(own, w_qkv, *after)


def row_blocks(me, own, orders, after):
    tokens, width = own.shape
    devices = len(orders[0])
    size = width // devices
    step = max(1, 16 // size)

    def kernel(me_ref, own_ref, *refs):
        out_refs, wide_ref = refs[len(after) : -1], refs[-1]
        for at in range(0, width, 2 * LANES):
            wide_ref[at : at + 2 * LANES, :] = own_ref[:, at : at + 2 * LANES].astype(F32).T
        me = me_ref[0]
        for i, order in enumerate(orders):
            for j in range(0, devices, step):
                rows = [
                    wide_ref[pl.ds(pl.multiple_of((me ^ int(order[k])) * size, size), size), :]
                    for k in range(j, j + step)
                ]
                half, base = divmod(j * size, width // 2)
                block = rows[0] if step == 1 else jnp.concatenate(rows, axis=0)
                out_refs[2 * i + half][base : base + step * size, :] = block.astype(BF)

    count = 2 * len(orders)
    out = pl.pallas_call(
        kernel,
        in_specs=[pl.BlockSpec(memory_space=pltpu.SMEM), pl.BlockSpec(memory_space=pltpu.VMEM)]
        + [pl.BlockSpec(memory_space=pl.ANY)] * len(after),
        out_specs=[pl.BlockSpec(memory_space=pltpu.VMEM)] * count,
        out_shape=[jax.ShapeDtypeStruct((width // 2, tokens), BF)] * count,
        scratch_shapes=[pltpu.VMEM((width, tokens), F32)],
        compiler_params=pltpu.CompilerParams(vmem_limit_bytes=16 * MIB),
        cost_estimate=pl.CostEstimate(flops=10**9, bytes_accessed=MIB, transcendentals=0),
    )(me, own, *after)
    return [out[2 * i : 2 * i + 2] for i in range(len(orders))]


def pack_sides(own, band_rows, band_cols):
    tokens, width = own.shape

    def kernel(own_ref, last_ref, first_ref, wide_ref):
        for lane, at in lanes_of(width):
            wide_ref[lane] = own_ref[:, at].astype(F32)
            for col in range(MARGIN):
                here = slice(col * band_rows, (col + 1) * band_rows)
                last = pl.ds(band_cols - MARGIN + col, band_rows, stride=band_cols)
                last_ref[here, at] = wide_ref[lane, last, :].astype(BF)
                first = pl.ds(col, band_rows, stride=band_cols)
                first_ref[here, at] = wide_ref[lane, first, :].astype(BF)

    out = ((MARGIN * band_rows, width), BF)
    scratch = [pltpu.VMEM((width // LANES, tokens, LANES), F32)]
    return on_chip(kernel, [out, out], [own], scratch=scratch)


def pack_rows(own, band_cols, after):
    tokens, width = own.shape
    edge = MARGIN * band_cols

    def kernel(own_ref, last_ref, first_ref):
        last_ref[...] = own_ref[tokens - edge :, :]
        first_ref[...] = own_ref[:edge, :]

    out = ((edge, width), BF)
    return on_chip(kernel, [out, out], [own], after=after)


def pack_corners(above, below, band_cols):
    edge, width = above.shape

    def kernel(above_ref, below_ref, last_ref, first_ref, wide_ref):
        wide_ref[:, edge:, :] = jnp.zeros_like(wide_ref[:, edge:, :])
        for rim, rim_ref in enumerate((above_ref, below_ref)):
            for lane, at in lanes_of(width):
                wide_ref[lane, :edge, :] = rim_ref[:, at].astype(F32)
                for out_ref, offset in ((last_ref, band_cols - MARGIN), (first_ref, 0)):
                    for col in range(0, MARGIN, 2):
                        base = (rim * MARGIN + col) * EDGE_R
                        pair = [
                            wide_ref[lane, pl.ds(offset + c, EDGE_R, stride=band_cols), :]
                            for c in (col, col + 1)
                        ]
                        out_ref[base : base + 2 * EDGE_R, at] = jnp.concatenate(pair).astype(BF)

    out = ((2 * MARGIN * EDGE_R, width), BF)
    scratch = [pltpu.VMEM((width // LANES, EDGE_R * band_cols, LANES), F32)]
    return on_chip(kernel, [out, out], [above, below], scratch=scratch)


def merge_sides(left, right, above, below, band_rows, band_cols, after=()):
    edge = MARGIN * band_cols

    def kernel(left_ref, right_ref, above_ref, below_ref, ol_ref, or_ref):
        for part in range(2):
            for col in range(2 * MARGIN):
                source, target = (left_ref, ol_ref) if col < MARGIN else (right_ref, or_ref)
                base = (col % MARGIN) * band_rows
                pair = slice(edge + (col // 2) * 2 * EDGE_R, edge + (col // 2 + 1) * 2 * EDGE_R)
                odd = slice((col % 2) * EDGE_R, (col % 2 + 1) * EDGE_R)
                rows = source[part, base : base + band_rows, :].astype(F32)
                first = rows[:EDGE_R] + above_ref[part, pair, :].astype(F32)[odd]
                last = rows[band_rows - EDGE_R :] + below_ref[part, pair, :].astype(F32)[odd]
                target[part, base : base + band_rows, :] = jnp.concatenate(
                    [first, rows[EDGE_R : band_rows - EDGE_R], last], axis=0
                ).astype(BF)

    out = [(left.shape, BF), (right.shape, BF)]
    return on_chip(kernel, out, [left, right, above, below], after=after)


def finish(mid, above, below, left, right, band_rows, band_cols, after, flops):
    _, tokens, width = mid.shape
    edge = MARGIN * band_cols

    def kernel(mid_ref, above_ref, below_ref, left_ref, right_ref, out_ref, acc_ref):
        for part in range(2):
            for block in range(width // (2 * LANES)):
                for lane in range(2):
                    at = slice((2 * block + lane) * LANES, (2 * block + lane + 1) * LANES)
                    acc_ref[lane] = mid_ref[part, :, at].astype(F32)
                    acc_ref[lane, :edge, :] += above_ref[part, :edge, at].astype(F32)
                    acc_ref[lane, tokens - edge :, :] += below_ref[part, :edge, at].astype(F32)
                    for col in range(MARGIN):
                        here = slice(col * band_rows, (col + 1) * band_rows)
                        first = pl.ds(col, band_rows, stride=band_cols)
                        last = pl.ds(band_cols - MARGIN + col, band_rows, stride=band_cols)
                        acc_ref[lane, first, :] += left_ref[part, here, at].astype(F32)
                        acc_ref[lane, last, :] += right_ref[part, here, at].astype(F32)
                both = jnp.concatenate([acc_ref[0], acc_ref[1]], axis=1).astype(BF)
                start = part * width + block * 2 * LANES
                out_ref[:, start : start + 2 * LANES] = both

    out = [((tokens, 2 * width), BF)]
    scratch = [pltpu.VMEM((2, tokens, LANES), F32)]
    operands = [mid, above, below, left, right]
    return on_chip(kernel, out, operands, after, scratch, flops)[0]


def grad_rows(rows, columns, scale, kind, after=()):
    features, width = rows[0].shape[0], columns.shape[1]

    def kernel(*refs):
        *rows_refs, columns_ref, out_ref = refs
        for start in range(0, width, 2 * LANES):
            here = slice(start, start + 2 * LANES)
            rows_ref = rows_refs[start * len(rows) // width]
            out_ref[:, here] = (dot(rows_ref[...], columns_ref[:, here]) * scale).astype(kind)

    return on_chip(kernel, [((features, width), kind)], [*rows, columns], after)[0]


def add_split(keep, received, after=(), parts=None):
    half, columns = keep.shape[0] // 2, keep.shape[1]
    parts = parts or len(received)
    part = columns // parts
    each = columns // len(received)

    def kernel(keep_ref, *refs):
        sums, *sends = refs[len(received) :]
        for i in range(parts):
            at = slice(i * part, (i + 1) * part)
            received_ref = refs[i * part // each]
            there = slice(i * part % each, i * part % each + part)
            sums[:, at] = keep_ref[:half, at] + received_ref[:half, there].astype(F32)
            sends[i][...] = (keep_ref[half:, at] + received_ref[half:, there].astype(F32)).astype(BF)

    out = [((half, columns), F32)] + [((half, part), BF)] * parts
    keep, *send = on_chip(kernel, out, [keep, *received], after=after)
    return keep, send


def add_blocks(keep, received, blocks):
    rows, columns = keep.shape
    part = columns // len(received)
    size = rows // blocks

    def kernel(keep_ref, *refs):
        sums, *send = refs[len(received) :]
        for i, received_ref in enumerate(refs[: len(received)]):
            at = slice(i * part, (i + 1) * part)
            total = keep_ref[:, at] + received_ref[...].astype(F32)
            sums[:, at] = total[:size]
            for b in range(1, blocks):
                send[b - 1][:, at] = total[b * size : (b + 1) * size].astype(BF)

    out = [((size, columns), F32)] + [((size, columns), BF)] * (blocks - 1)
    keep, *send = on_chip(kernel, out, [keep, *received])
    return keep, send


def gather_sums(groups, places, width):
    flat = [a for group in groups for a in group]

    def kernel(*refs):
        out_ref = refs[-1]
        at = 0
        for group, moves in zip(groups, places):
            total = refs[at][...]
            for ref in refs[at + 1 : at + len(group)]:
                total = total + ref[...].astype(F32)
            at += len(group)
            for source, size, target in moves:
                out_ref[:, target : target + size] = total[:, source : source + size]

    return on_chip(kernel, [((flat[0].shape[0], width), F32)], flat)[0]


def shifted(array, axis, by, wrap):
    size = lax.axis_size(axis)
    route = [(i, (i + by) % size) for i in range(size) if wrap or 0 <= i + by < size]
    return lax.ppermute(array, axis, route)


def exchanged(array, axis, flip):
    return lax.ppermute(array, axis, [(i, i ^ flip) for i in range(lax.axis_size(axis))])


def bits_of(axis):
    return [(axis, 1 << b) for b in range((lax.axis_size(axis) - 1).bit_length())]


def feature_order(stages):
    n_lon, n_lat = lax.axis_size("lon"), lax.axis_size("lat")
    unit = {"lon": 1, "lat": n_lon, "dp": n_lon * n_lat}
    order = np.arange(n_lon)
    for axis, bit in reversed(stages):
        order = np.concatenate([order, order + unit[axis] * bit])
    return order.astype(np.int32)


def body(inputs, grad_out, w_qkv):
    _, band_rows, band_cols, width = inputs.shape
    n_lat, n_lon, n_dp = lax.axis_size("lat"), lax.axis_size("lon"), lax.axis_size("dp")
    band_start = lax.axis_index("lat") * band_rows
    total_rows = band_rows * n_lat
    tokens = band_rows * band_cols
    slots = HEADS // GROUP // 2
    shape = (band_rows, band_cols, total_rows)
    own = inputs.reshape(tokens, width)
    flat_grad = grad_out.reshape(tokens, width)

    last_cols, first_cols = pack_sides(own, band_rows, band_cols)
    left = shifted(last_cols, "lon", 1, True)
    right = shifted(first_cols, "lon", -1, True)
    last_rows, first_rows = pack_rows(own, band_cols, [last_cols])
    above = shifted(last_rows, "lat", 1, False)
    below = shifted(first_rows, "lat", -1, False)
    last_corners, first_corners = pack_corners(above, below, band_cols)
    corner_left = shifted(last_corners, "lon", 1, True)
    corner_right = shifted(first_corners, "lon", -1, True)
    halo = (left, right, above, below, corner_left, corner_right)

    start = band_start.reshape(1)
    masks = window_masks(start, band_rows, band_cols, total_rows)
    qkv = project(own, w_qkv, [last_corners])
    lat_bits = bits_of("lat")
    x_first = lat_bits[:1] + bits_of("dp") + lat_bits[1:]
    y_first = lat_bits + bits_of("dp")
    me = (lax.axis_index("dp") * n_lat + lax.axis_index("lat")) * n_lon + lax.axis_index("lon")
    half = width // 2
    rows_x, rows_y = row_blocks(
        me.reshape(1), own, [feature_order(x_first), feature_order(y_first)], [last_corners]
    )
    scale = float(tokens * n_dp * n_lat * n_lon) ** -0.5

    attend = lambda first, count, before, after: attention_grads(
        first, count, slots, start, masks, halo, qkv, flat_grad, w_qkv, shape, before, after
    )

    def return_rows(grads):
        from_below = shifted(grads[1], "lat", -1, False)
        from_above = shifted(grads[2], "lat", 1, False)
        return from_above, from_below

    def return_sides(grads, rims, after):
        to_left, to_right = merge_sides(grads[4], grads[5], *rims, band_rows, band_cols, after)
        from_right = shifted(to_left, "lon", -1, True)
        from_left = shifted(to_right, "lon", 1, True)
        return to_left, from_left, from_right

    one = attend(0, slots, [], [*rows_x, *rows_y])
    rims_1 = return_rows(one)
    two = attend(slots, 1, [(0, one[0])], [])
    sent, *sides_1 = return_sides(one, rims_1, [two[1]])
    two = attend(slots + 1, 1, list(enumerate(two)), [sent])
    rims_2 = return_rows(two)
    dq = two[0]

    send_q = grad_rows([rows_x[1]], dq, scale, BF, after=sides_1)
    keep_q = dot(rows_x[0], dq) * scale
    sent, *sides_2 = return_sides(two, rims_2, [send_q])
    dkv_1 = finish(one[3], *rims_1, *sides_1, band_rows, band_cols, [sent], 10**5)
    send_1 = grad_rows([rows_y[1]], dkv_1, scale, BF)
    keep_1 = dot(rows_y[0], dkv_1) * scale
    received = [exchanged(send_q, *x_first[0]), exchanged(send_1, *y_first[0])]
    keep, send = add_split(jnp.concatenate([keep_q, keep_1], axis=1), received)

    dkv_2 = finish(two[3], *rims_2, *sides_2, band_rows, band_cols, [keep], FINISH_FLOPS)
    for step_x, step_y in zip(x_first[1:-1], y_first[1:-1]):
        received = [exchanged(send[0], *step_x), exchanged(send[1], *step_y)]
        keep, send = add_split(keep, received, [dkv_2])
    send_2 = grad_rows((rows_x[1], rows_y[1]), dkv_2, scale, BF, after=[keep])
    received_2 = [exchanged(send_2, *x_first[0])]
    keep_2 = grad_rows((rows_x[0], rows_y[0]), dkv_2, scale, F32, after=[keep])
    received = [exchanged(send[0], *x_first[-1]), exchanged(send[1], *y_first[-1])]
    keep, send = add_blocks(keep, received, n_lon)
    group_1 = [keep] + [exchanged(a, "lon", i + 1) for i, a in enumerate(send)]
    for step_x, step_y in zip(x_first[1:], y_first[1:]):
        keep_2, send = add_split(keep_2, received_2, parts=2)
        received_2 = [exchanged(send[0], *step_x), exchanged(send[1], *step_y)]
    keep_2, send = add_blocks(keep_2, received_2, n_lon)
    group_2 = [keep_2] + [exchanged(a, "lon", i + 1) for i, a in enumerate(send)]
    places = [
        [(0, width, 0), (width, half, width), (width + half, half, 2 * width)],
        [(0, half, width + half), (half, half, 2 * width + half)],
    ]
    grad_w = gather_sums([group_1, group_2], places, 3 * width)

    grad_proj = jnp.concatenate(
        [dq, dkv_1[:, :half], dkv_2[:, :half], dkv_1[:, half:], dkv_2[:, half:]], axis=1
    )
    grad_inputs = dot(grad_proj, w_qkv, NT).astype(BF).reshape(inputs.shape)
    return (grad_inputs, grad_w)


def solution(mesh):
    in_specs = (P("dp", "lat", "lon", None), P("dp", "lat", "lon", None), P())
    out_specs = (P("dp", "lat", "lon", None), P(("dp", "lat", "lon"), None))
    return jax.shard_map(body, mesh=mesh, in_specs=in_specs, out_specs=out_specs, check_vma=False)
```

profile of v0, /device:TPU:0, one launch (start us, length us, event | category | flops | bytes accessed | tf_op | source)
XLA Modules:
  0.0 163.2 jit_solution(11496878509682567286)
XLA Ops:
  2.7 2.4 %collective-permute-start.2 = (bf16[96,1024]{1,0:T(8,128)(2,1)S(1)}, bf16[96,1024]{1,0:T(8,128)(2,1)S(1)}, u32[]{:S(2)}, u32[]{:S(2)}) collective-permute-start(bf16[96,1024]{1,0:T(8,128)(2,1)S(1)} %get-tuple-element.56), channel_id=1, source_target_pairs={{0,4},{4,8},{8,12},{1,5},{5,9},{9,13},{2,6},{6,10},{10,14},{3,7},{... | collective-permute-start | bytes 589832 | tf_op jit(solution)/shard_map/ppermute | solution.py:567
  6.3 4.5 %collective-permute-start.1 = (bf16[192,1024]{1,0:T(8,128)(2,1)S(1)}, bf16[192,1024]{1,0:T(8,128)(2,1)S(1)}, u32[]{:S(2)}, u32[]{:S(2)}) collective-permute-start(bf16[192,1024]{1,0:T(8,128)(2,1)S(1)} %get-tuple-element.55), channel_id=1, source_target_pairs={{0,3},{1,0},{2,1},{3,2},{4,7},{5,4},{6,5},{7,6},{8,11},{9,8},{10,9... | collective-permute-start | bytes 1179656 | tf_op jit(solution)/shard_map/ppermute | solution.py:567
  11.8 3.8 %collective-permute-start.5 = (bf16[96,1024]{1,0:T(8,128)(2,1)}, bf16[96,1024]{1,0:T(8,128)(2,1)S(1)}, u32[]{:S(2)}, u32[]{:S(2)}) collective-permute-start(bf16[96,1024]{1,0:T(8,128)(2,1)} %get-tuple-element.59), channel_id=1, source_target_pairs={{0,3},{1,0},{2,1},{3,2},{4,7},{5,4},{6,5},{7,6},{8,11},{9,8},{10,9... | collective-permute-start | bytes 589832 | tf_op jit(solution)/shard_map/ppermute | solution.py:567
  15.6 3.3 %shard_map.50.refs_1_ = bf16[8,512,128]{2,1,0:T(8,128)(2,1)} custom-call(s32[1]{0:T(128)} %bitcast.start_ref.refs_0_), custom_call_target="tpu_custom_call" | custom-call | flops 10000000 | bytes 2097152 | tf_op jit(solution)/shard_map/pallas_call | solution.py:68
  19.5 2.8 %copy-done.2 = bf16[1024,3072]{1,0:T(8,128)(2,1)S(1)} copy-done((bf16[1024,3072]{1,0:T(8,128)(2,1)S(1)}, bf16[1024,3072]{1,0:T(8,128)(2,1)}, u32[]{:S(2)}) %copy-start.2) | copy-done | bytes 6291480
  22.3 4.9 %shard_map.54.refs_8_ = bf16[512,3072]{1,0:T(8,128)(2,1)S(1)} custom-call(bf16[512,1024]{1,0:T(8,128)(2,1)S(1)} %bitcast.14, bf16[1024,3072]{1,0:T(8,128)(2,1)S(1)} %copy-done.2, bf16[96,1024]{1,0:T(8,128)(2,1)S(1)} %get-tuple-element.58.refs_0_), custom_call_target="tpu_custom_call" | custom-call | flops 1000000000 | bytes 1048576 | tf_op jit(solution)/shard_map/pallas_call | solution.py:344
  27.2 4.5 %collective-permute-done.5.refs_7_ = bf16[96,1024]{1,0:T(8,128)(2,1)S(1)} collective-permute-done((bf16[96,1024]{1,0:T(8,128)(2,1)}, bf16[96,1024]{1,0:T(8,128)(2,1)S(1)}, u32[]{:S(2)}, u32[]{:S(2)}) %collective-permute-start.5) | collective-permute-done | bytes 196640 | tf_op jit(solution)/shard_map/ppermute | solution.py:567
  31.7 5.0 %collective-permute-done.4.refs_6_ = bf16[96,1024]{1,0:T(8,128)(2,1)} collective-permute-done((bf16[96,1024]{1,0:T(8,128)(2,1)S(1)}, bf16[96,1024]{1,0:T(8,128)(2,1)}, u32[]{:S(2)}, u32[]{:S(2)}) %collective-permute-start.4) | collective-permute-done | bytes 196640 | tf_op jit(solution)/shard_map/ppermute | solution.py:567
  36.8 2.8 %copy-done.3 = bf16[1024,3072]{1,0:T(8,128)(2,1)S(1)} copy-done((bf16[1024,3072]{1,0:T(8,128)(2,1)S(1)}, bf16[1024,3072]{1,0:T(8,128)(2,1)}, u32[]{:S(2)}) %copy-start.3) | copy-done | bytes 6291480
  39.5 17.6 %shard_map.56 = (bf16[512,1024]{1,0:T(8,128)(2,1)S(1)}, bf16[2,192,512]{2,1,0:T(8,128)(2,1)S(1)}, bf16[2,192,512]{2,1,0:T(8,128)(2,1)S(1)}, bf16[2,512,512]{2,1,...) custom-call(s32[1]{0:T(128)} %bitcast.start_ref.refs_0_, ...), custom_call_target="tpu_custom_call" | custom-call | flops 28000000000 | bytes 16777216 | tf_op jit(solution)/shard_map/pallas_call | solution.py:275
  57.1 3.3 %collective-permute-start.6 = (bf16[2,192,512]{2,1,0:T(8,128)(2,1)S(1)}, bf16[2,192,512]{2,1,0:T(8,128)(2,1)S(1)}, u32[]{:S(2)}, u32[]{:S(2)}) collective-permute-start(bf16[2,192,512]{2,1,0:T(8,128)(2,1)S(1)} %get-tuple-element.73), channel_id=1, source_target_pairs={{0,4},{4,8},{8,12},{1,5},{5,9},{9,13},{2,6},{6,10},{10,14},{3,7},{... | collective-permute-start | bytes 1179656 | tf_op jit(solution)/shard_map/ppermute | solution.py:567
  61.9 9.3 %shard_map.57 = (bf16[512,1024]{1,0:T(8,128)(2,1)S(1)}, bf16[2,192,512]{2,1,0:T(8,128)(2,1)S(1)}, bf16[2,192,512]{2,1,0:T(8,128)(2,1)S(1)}, bf16[2,512,512]{2,1,...) custom-call(s32[1]{0:T(128)} %bitcast.start_ref.refs_0_, ...), custom_call_target="tpu_custom_call", output_to_operand_aliasing={{0}: (11, {})} | custom-call | flops 14000000000 | bytes 8388608 | tf_op jit(solution)/shard_map/pallas_call | solution.py:275
  73.0 2.2 %collective-permute-start.9 = (bf16[2,192,512]{2,1,0:T(8,128)(2,1)S(1)}, bf16[2,192,512]{2,1,0:T(8,128)(2,1)S(1)}, u32[]{:S(2)}, u32[]{:S(2)}) collective-permute-start(bf16[2,192,512]{2,1,0:T(8,128)(2,1)S(1)} %get-tuple-element.75.refs_17_), channel_id=1, source_target_pairs={{0,3},{1,0},{2,1},{3,2},{4,7},{5,4},{6,5},{7,6},{8,11},{9,8},{10,9... | collective-permute-start | bytes 1179656 | tf_op jit(solution)/shard_map/ppermute | solution.py:567
  75.2 9.3 %shard_map.59 = (bf16[512,1024]{1,0:T(8,128)(2,1)S(1)}, bf16[2,192,512]{2,1,0:T(8,128)(2,1)S(1)}, bf16[2,192,512]{2,1,0:T(8,128)(2,1)S(1)}, bf16[2,512,512]{2,1,...) custom-call(s32[1]{0:T(128)} %bitcast.start_ref.refs_0_, ...), custom_call_target="tpu_custom_call", output_to_operand_aliasing={{0}: (11, {}), {1}: (12, {}), {2}: (13, {}), {3}: (14, {}),... | custom-call | flops 14000000000 | bytes 8388608 | tf_op jit(solution)/shard_map/pallas_call | solution.py:275
  84.5 4.1 %collective-permute-start.10 = (bf16[2,192,512]{2,1,0:T(8,128)(2,1)S(1)}, bf16[2,192,512]{2,1,0:T(8,128)(2,1)S(1)}, u32[]{:S(2)}, u32[]{:S(2)}) collective-permute-start(bf16[2,192,512]{2,1,0:T(8,128)(2,1)S(1)} %get-tuple-element.81), channel_id=1, source_target_pairs={{0,4},{4,8},{8,12},{1,5},{5,9},{9,13},{2,6},{6,10},{10,14},{3,7},{... | collective-permute-start | bytes 1179656 | tf_op jit(solution)/shard_map/ppermute | solution.py:567
  90.1 2.9 %collective-permute-done.9.refs_3_.refs_4_ = bf16[2,192,512]{2,1,0:T(8,128)(2,1)S(1)} collective-permute-done((bf16[2,192,512]{2,1,0:T(8,128)(2,1)S(1)}, bf16[2,192,512]{2,1,0:T(8,128)(2,1)S(1)}, u32[]{:S(2)}, u32[]{:S(2)}) %collective-permute-start.9) | collective-permute-done | bytes 393248 | tf_op jit(solution)/shard_map/ppermute | solution.py:567
  96.2 6.0 %collective-permute-start.15 = (bf16[512,1024]{1,0:T(8,128)(2,1)S(1)}, bf16[512,1024]{1,0:T(8,128)(2,1)S(1)}, u32[]{:S(2)}, u32[]{:S(2)}) collective-permute-start(bf16[512,1024]{1,0:T(8,128)(2,1)S(1)} %shard_map.63), channel_id=1, source_target_pairs={{0,4},{4,0},{8,12},{12,8},{1,5},{5,1},{9,13},{13,9},{2,6},{6,2},{1... | collective-permute-start | bytes 3145736 | tf_op jit(solution)/shard_map/ppermute | solution.py:571
  103.1 2.0 %collective-permute-start.12 = (bf16[2,192,512]{2,1,0:T(8,128)(2,1)S(1)}, bf16[2,192,512]{2,1,0:T(8,128)(2,1)S(1)}, u32[]{:S(2)}, u32[]{:S(2)}) collective-permute-start(bf16[2,192,512]{2,1,0:T(8,128)(2,1)S(1)} %get-tuple-element.85), channel_id=1, source_target_pairs={{0,1},{1,2},{2,3},{3,0},{4,5},{5,6},{6,7},{7,4},{8,9},{9,10},{10,1... | collective-permute-start | bytes 1179656 | tf_op jit(solution)/shard_map/ppermute | solution.py:567
  108.4 13.4 %collective-permute-done.12.refs_3_ = bf16[2,192,512]{2,1,0:T(8,128)(2,1)S(1)} collective-permute-done((bf16[2,192,512]{2,1,0:T(8,128)(2,1)S(1)}, bf16[2,192,512]{2,1,0:T(8,128)(2,1)S(1)}, u32[]{:S(2)}, u32[]{:S(2)}) %collective-permute-start.12) | collective-permute-done | bytes 393248 | tf_op jit(solution)/shard_map/ppermute | solution.py:567
  130.6 4.7 %collective-permute-done.18.refs_1_ = bf16[128,1024]{1,0:T(8,128)(2,1)S(1)} collective-permute-done((bf16[128,1024]{1,0:T(8,128)(2,1)S(1)}, bf16[128,1024]{1,0:T(8,128)(2,1)S(1)}, u32[]{:S(2)}, u32[]{:S(2)}) %collective-permute-start.18) | collective-permute-done | bytes 262176 | tf_op jit(solution)/shard_map/ppermute | solution.py:571
  135.9 4.7 %collective-permute-done.24.refs_1_ = bf16[256,512]{1,0:T(8,128)(2,1)S(1)} collective-permute-done((bf16[256,512]{1,0:T(8,128)(2,1)S(1)}, bf16[256,512]{1,0:T(8,128)(2,1)S(1)}, u32[]{:S(2)}, u32[]{:S(2)}) %collective-permute-start.24) | collective-permute-done | bytes 262176 | tf_op jit(solution)/shard_map/ppermute | solution.py:571
  149.7 2.2 %collective-permute-start.30 = (bf16[32,1024]{1,0:T(8,128)(2,1)S(1)}, bf16[32,1024]{1,0:T(8,128)(2,1)S(1)}, u32[]{:S(2)}, u32[]{:S(2)}) collective-permute-start(bf16[32,1024]{1,0:T(8,128)(2,1)S(1)} %get-tuple-element.105), channel_id=1, source_target_pairs={{0,3},{1,2},{2,1},{3,0},{4,7},{5,6},{6,5},{7,4},{8,11},{9,10},{10,... | collective-permute-start | bytes 196616 | tf_op jit(solution)/shard_map/ppermute | solution.py:571
  151.9 4.4 %convolution_convert_fusion = bf16[512,1024]{1,0:T(8,128)(2,1)} fusion(bf16[512,3072]{1,0:T(8,128)(2,1)S(1)} %slice_dynamic-update-slice_fusion, bf16[1024,3072]{1,0:T(8,128)(2,1)S(1)} %bitcast.16), kind=kOutput, calls=%fused_computation.3 | convolution fusion | flops 3221749760 | bytes 10485760 | tf_op jit(solution)/shard_map/dot_general | solution.py:34
  158.2 4.2 %collective-permute-done.29.refs_6_ = bf16[32,1024]{1,0:T(8,128)(2,1)S(1)} collective-permute-done((bf16[32,1024]{1,0:T(8,128)(2,1)S(1)}, bf16[32,1024]{1,0:T(8,128)(2,1)S(1)}, u32[]{:S(2)}, u32[]{:S(2)}) %collective-permute-start.29) | collective-permute-done | bytes 65568 | tf_op jit(solution)/shard_map/ppermute | solution.py:571
  (88 shorter events, 37.9 us)
Async XLA Ops:
  6.3 30.4 %collective-permute-start.1 = (bf16[192,1024]{1,0:T(8,128)(2,1)S(1)}, bf16[192,1024]{1,0:T(8,128)(2,1)S(1)}, u32[]{:S(2)}, u32[]{:S(2)}) collective-permute-start(bf16[192,1024]{1,0:T(8,128)(2,1)S(1)} %get-tuple-element.55), channel_id=1, source_target_pairs={{0,3},{1,0},{2,1},{3,2},{4,7},{5,4},{6,5},{7,6},{8,11},{9,8},{10,9... | collective-permute-start | bytes 1179656 | tf_op jit(solution)/shard_map/ppermute | solution.py:567
  10.8 25.9 %collective-permute-start = (bf16[192,1024]{1,0:T(8,128)(2,1)S(1)}, bf16[192,1024]{1,0:T(8,128)(2,1)S(1)}, u32[]{:S(2)}, u32[]{:S(2)}) collective-permute-start(bf16[192,1024]{1,0:T(8,128)(2,1)S(1)} %get-tuple-element.54.refs_1_), channel_id=1, source_target_pairs={{0,1},{1,2},{2,3},{3,0},{4,5},{5,6},{6,7},{7,4},{8,9},{9,10},{10,1... | collective-permute-start | bytes 1179656 | tf_op jit(solution)/shard_map/ppermute | solution.py:567
  11.8 19.9 %collective-permute-start.5 = (bf16[96,1024]{1,0:T(8,128)(2,1)}, bf16[96,1024]{1,0:T(8,128)(2,1)S(1)}, u32[]{:S(2)}, u32[]{:S(2)}) collective-permute-start(bf16[96,1024]{1,0:T(8,128)(2,1)} %get-tuple-element.59), channel_id=1, source_target_pairs={{0,3},{1,0},{2,1},{3,2},{4,7},{5,4},{6,5},{7,6},{8,11},{9,8},{10,9... | collective-permute-start | bytes 589832 | tf_op jit(solution)/shard_map/ppermute | solution.py:567
  15.6 21.1 %collective-permute-start.4 = (bf16[96,1024]{1,0:T(8,128)(2,1)S(1)}, bf16[96,1024]{1,0:T(8,128)(2,1)}, u32[]{:S(2)}, u32[]{:S(2)}) collective-permute-start(bf16[96,1024]{1,0:T(8,128)(2,1)S(1)} %get-tuple-element.58.refs_0_), channel_id=1, source_target_pairs={{0,1},{1,2},{2,3},{3,0},{4,5},{5,6},{6,7},{7,4},{8,9},{9,10},{10,1... | collective-permute-start | bytes 589832 | tf_op jit(solution)/shard_map/ppermute | solution.py:567
  57.1 14.0 %collective-permute-start.6 = (bf16[2,192,512]{2,1,0:T(8,128)(2,1)S(1)}, bf16[2,192,512]{2,1,0:T(8,128)(2,1)S(1)}, u32[]{:S(2)}, u32[]{:S(2)}) collective-permute-start(bf16[2,192,512]{2,1,0:T(8,128)(2,1)S(1)} %get-tuple-element.73), channel_id=1, source_target_pairs={{0,4},{4,8},{8,12},{1,5},{5,9},{9,13},{2,6},{6,10},{10,14},{3,7},{... | collective-permute-start | bytes 1179656 | tf_op jit(solution)/shard_map/ppermute | solution.py:567
  60.4 10.8 %collective-permute-start.7 = (bf16[2,192,512]{2,1,0:T(8,128)(2,1)S(1)}, bf16[2,192,512]{2,1,0:T(8,128)(2,1)S(1)}, u32[]{:S(2)}, u32[]{:S(2)}) collective-permute-start(bf16[2,192,512]{2,1,0:T(8,128)(2,1)S(1)} %get-tuple-element.74), channel_id=1, source_target_pairs={{4,0},{8,4},{12,8},{5,1},{9,5},{13,9},{6,2},{10,6},{14,10},{7,3},{... | collective-permute-start | bytes 1179656 | tf_op jit(solution)/shard_map/ppermute | solution.py:567
  71.3 18.8 %collective-permute-start.8 = (bf16[2,192,512]{2,1,0:T(8,128)(2,1)S(1)}, bf16[2,192,512]{2,1,0:T(8,128)(2,1)S(1)}, u32[]{:S(2)}, u32[]{:S(2)}) collective-permute-start(bf16[2,192,512]{2,1,0:T(8,128)(2,1)S(1)} %get-tuple-element.78), channel_id=1, source_target_pairs={{0,1},{1,2},{2,3},{3,0},{4,5},{5,6},{6,7},{7,4},{8,9},{9,10},{10,1... | collective-permute-start | bytes 1179656 | tf_op jit(solution)/shard_map/ppermute | solution.py:567
  73.0 20.1 %collective-permute-start.9 = (bf16[2,192,512]{2,1,0:T(8,128)(2,1)S(1)}, bf16[2,192,512]{2,1,0:T(8,128)(2,1)S(1)}, u32[]{:S(2)}, u32[]{:S(2)}) collective-permute-start(bf16[2,192,512]{2,1,0:T(8,128)(2,1)S(1)} %get-tuple-element.75.refs_17_), channel_id=1, source_target_pairs={{0,3},{1,0},{2,1},{3,2},{4,7},{5,4},{6,5},{7,6},{8,11},{9,8},{10,9... | collective-permute-start | bytes 1179656 | tf_op jit(solution)/shard_map/ppermute | solution.py:567
  84.5 9.3 %collective-permute-start.10 = (bf16[2,192,512]{2,1,0:T(8,128)(2,1)S(1)}, bf16[2,192,512]{2,1,0:T(8,128)(2,1)S(1)}, u32[]{:S(2)}, u32[]{:S(2)}) collective-permute-start(bf16[2,192,512]{2,1,0:T(8,128)(2,1)S(1)} %get-tuple-element.81), channel_id=1, source_target_pairs={{0,4},{4,8},{8,12},{1,5},{5,9},{9,13},{2,6},{6,10},{10,14},{3,7},{... | collective-permute-start | bytes 1179656 | tf_op jit(solution)/shard_map/ppermute | solution.py:567
  96.2 10.2 %collective-permute-start.15 = (bf16[512,1024]{1,0:T(8,128)(2,1)S(1)}, bf16[512,1024]{1,0:T(8,128)(2,1)S(1)}, u32[]{:S(2)}, u32[]{:S(2)}) collective-permute-start(bf16[512,1024]{1,0:T(8,128)(2,1)S(1)} %shard_map.63), channel_id=1, source_target_pairs={{0,4},{4,0},{8,12},{12,8},{1,5},{5,1},{9,13},{13,9},{2,6},{6,2},{1... | collective-permute-start | bytes 3145736 | tf_op jit(solution)/shard_map/ppermute | solution.py:571
  103.0 19.9 %collective-permute-start.13 = (bf16[2,192,512]{2,1,0:T(8,128)(2,1)S(1)}, bf16[2,192,512]{2,1,0:T(8,128)(2,1)S(1)}, u32[]{:S(2)}, u32[]{:S(2)}) collective-permute-start(bf16[2,192,512]{2,1,0:T(8,128)(2,1)S(1)} %get-tuple-element.83.refs_5_), channel_id=1, source_target_pairs={{0,3},{1,0},{2,1},{3,2},{4,7},{5,4},{6,5},{7,6},{8,11},{9,8},{10,9... | collective-permute-start | bytes 1179656 | tf_op jit(solution)/shard_map/ppermute | solution.py:567
  103.1 18.7 %collective-permute-start.12 = (bf16[2,192,512]{2,1,0:T(8,128)(2,1)S(1)}, bf16[2,192,512]{2,1,0:T(8,128)(2,1)S(1)}, u32[]{:S(2)}, u32[]{:S(2)}) collective-permute-start(bf16[2,192,512]{2,1,0:T(8,128)(2,1)S(1)} %get-tuple-element.85), channel_id=1, source_target_pairs={{0,1},{1,2},{2,3},{3,0},{4,5},{5,6},{6,7},{7,4},{8,9},{9,10},{10,1... | collective-permute-start | bytes 1179656 | tf_op jit(solution)/shard_map/ppermute | solution.py:567
  106.7 17.5 %collective-permute-start.16 = (bf16[256,1024]{1,0:T(8,128)(2,1)S(1)}, bf16[256,1024]{1,0:T(8,128)(2,1)S(1)}, u32[]{:S(2)}, u32[]{:S(2)}) collective-permute-start(bf16[256,1024]{1,0:T(8,128)(2,1)S(1)} %get-tuple-element.87), channel_id=1, source_target_pairs={{0,16},{16,0},{1,17},{17,1},{2,18},{18,2},{3,19},{19,3},{4,20},{20... | collective-permute-start | bytes 1572872 | tf_op jit(solution)/shard_map/ppermute | solution.py:571
  108.3 16.0 %collective-permute-start.17 = (bf16[256,1024]{1,0:T(8,128)(2,1)S(1)}, bf16[256,1024]{1,0:T(8,128)(2,1)S(1)}, u32[]{:S(2)}, u32[]{:S(2)}) collective-permute-start(bf16[256,1024]{1,0:T(8,128)(2,1)S(1)} %get-tuple-element.88), channel_id=1, source_target_pairs={{0,8},{4,12},{8,0},{12,4},{1,9},{5,13},{9,1},{13,5},{2,10},{6,14},... | collective-permute-start | bytes 1572872 | tf_op jit(solution)/shard_map/ppermute | solution.py:571
  126.2 9.2 %collective-permute-start.18 = (bf16[128,1024]{1,0:T(8,128)(2,1)S(1)}, bf16[128,1024]{1,0:T(8,128)(2,1)S(1)}, u32[]{:S(2)}, u32[]{:S(2)}) collective-permute-start(bf16[128,1024]{1,0:T(8,128)(2,1)S(1)} %get-tuple-element.90), channel_id=1, source_target_pairs={{0,8},{4,12},{8,0},{12,4},{1,9},{5,13},{9,1},{13,5},{2,10},{6,14},... | collective-permute-start | bytes 786440 | tf_op jit(solution)/shard_map/ppermute | solution.py:571
  126.3 9.2 %collective-permute-start.19 = (bf16[128,1024]{1,0:T(8,128)(2,1)S(1)}, bf16[128,1024]{1,0:T(8,128)(2,1)S(1)}, u32[]{:S(2)}, u32[]{:S(2)}) collective-permute-start(bf16[128,1024]{1,0:T(8,128)(2,1)S(1)} %get-tuple-element.91), channel_id=1, source_target_pairs={{0,16},{16,0},{1,17},{17,1},{2,18},{18,2},{3,19},{19,3},{4,20},{20... | collective-permute-start | bytes 786440 | tf_op jit(solution)/shard_map/ppermute | solution.py:571
  128.1 12.5 %collective-permute-start.24 = (bf16[256,512]{1,0:T(8,128)(2,1)S(1)}, bf16[256,512]{1,0:T(8,128)(2,1)S(1)}, u32[]{:S(2)}, u32[]{:S(2)}) collective-permute-start(bf16[256,512]{1,0:T(8,128)(2,1)S(1)} %get-tuple-element.97), channel_id=1, source_target_pairs={{0,16},{16,0},{1,17},{17,1},{2,18},{18,2},{3,19},{19,3},{4,20},{20... | collective-permute-start | bytes 786440 | tf_op jit(solution)/shard_map/ppermute | solution.py:571
  129.7 11.0 %collective-permute-start.25 = (bf16[256,512]{1,0:T(8,128)(2,1)S(1)}, bf16[256,512]{1,0:T(8,128)(2,1)S(1)}, u32[]{:S(2)}, u32[]{:S(2)}) collective-permute-start(bf16[256,512]{1,0:T(8,128)(2,1)S(1)} %get-tuple-element.98), channel_id=1, source_target_pairs={{0,8},{4,12},{8,0},{12,4},{1,9},{5,13},{9,1},{13,5},{2,10},{6,14},... | collective-permute-start | bytes 786440 | tf_op jit(solution)/shard_map/ppermute | solution.py:571
  135.5 14.2 %collective-permute-start.20 = (bf16[32,2048]{1,0:T(8,128)(2,1)S(1)}, bf16[32,2048]{1,0:T(8,128)(2,1)S(1)}, u32[]{:S(2)}, u32[]{:S(2)}) collective-permute-start(bf16[32,2048]{1,0:T(8,128)(2,1)S(1)} %get-tuple-element.93), channel_id=1, source_target_pairs={{0,1},{1,0},{2,3},{3,2},{4,5},{5,4},{6,7},{7,6},{8,9},{9,8},{10,11... | collective-permute-start | bytes 393224 | tf_op jit(solution)/shard_map/ppermute | solution.py:571
  144.0 14.2 %collective-permute-start.21 = (bf16[32,2048]{1,0:T(8,128)(2,1)S(1)}, bf16[32,2048]{1,0:T(8,128)(2,1)S(1)}, u32[]{:S(2)}, u32[]{:S(2)}) collective-permute-start(bf16[32,2048]{1,0:T(8,128)(2,1)S(1)} %get-tuple-element.94), channel_id=1, source_target_pairs={{0,2},{1,3},{2,0},{3,1},{4,6},{5,7},{6,4},{7,5},{8,10},{9,11},{10,... | collective-permute-start | bytes 393224 | tf_op jit(solution)/shard_map/ppermute | solution.py:571
  145.2 12.9 %collective-permute-start.22 = (bf16[32,2048]{1,0:T(8,128)(2,1)S(1)}, bf16[32,2048]{1,0:T(8,128)(2,1)S(1)}, u32[]{:S(2)}, u32[]{:S(2)}) collective-permute-start(bf16[32,2048]{1,0:T(8,128)(2,1)S(1)} %get-tuple-element.95), channel_id=1, source_target_pairs={{0,3},{1,2},{2,1},{3,0},{4,7},{5,6},{6,5},{7,4},{8,11},{9,10},{10,... | collective-permute-start | bytes 393224 | tf_op jit(solution)/shard_map/ppermute | solution.py:571
  147.5 10.7 %collective-permute-start.28 = (bf16[32,1024]{1,0:T(8,128)(2,1)S(1)}, bf16[32,1024]{1,0:T(8,128)(2,1)S(1)}, u32[]{:S(2)}, u32[]{:S(2)}) collective-permute-start(bf16[32,1024]{1,0:T(8,128)(2,1)S(1)} %get-tuple-element.103), channel_id=1, source_target_pairs={{0,1},{1,0},{2,3},{3,2},{4,5},{5,4},{6,7},{7,6},{8,9},{9,8},{10,11... | collective-permute-start | bytes 196616 | tf_op jit(solution)/shard_map/ppermute | solution.py:571
  147.9 14.5 %collective-permute-start.29 = (bf16[32,1024]{1,0:T(8,128)(2,1)S(1)}, bf16[32,1024]{1,0:T(8,128)(2,1)S(1)}, u32[]{:S(2)}, u32[]{:S(2)}) collective-permute-start(bf16[32,1024]{1,0:T(8,128)(2,1)S(1)} %get-tuple-element.104), channel_id=1, source_target_pairs={{0,2},{1,3},{2,0},{3,1},{4,6},{5,7},{6,4},{7,5},{8,10},{9,11},{10,... | collective-permute-start | bytes 196616 | tf_op jit(solution)/shard_map/ppermute | solution.py:571
  149.7 12.6 %collective-permute-start.30 = (bf16[32,1024]{1,0:T(8,128)(2,1)S(1)}, bf16[32,1024]{1,0:T(8,128)(2,1)S(1)}, u32[]{:S(2)}, u32[]{:S(2)}) collective-permute-start(bf16[32,1024]{1,0:T(8,128)(2,1)S(1)} %get-tuple-element.105), channel_id=1, source_target_pairs={{0,3},{1,2},{2,1},{3,0},{4,7},{5,6},{6,5},{7,4},{8,11},{9,10},{10,... | collective-permute-start | bytes 196616 | tf_op jit(solution)/shard_map/ppermute | solution.py:571
  (15 other events, 142.2 us)
where the time goes:
time: 164 us; the launch traced here: 163 us
  Pallas kernels  54.2 us (33%)
  starting transfers between devices  51 us (31%)
  waiting for transfers between devices  43.6 us (27%)
  local copies, waits for them, and re-layouts  7.02 us (4%)
  matrix products  5.86 us (4%)
    pallas_call x3, Pallas kernels, attention_grads(): pl.pallas_call(functools.partial(attention_kernel, band_rows, band_cols,...  36.1 us
    ppermute x14, starting transfers between devices, shifted(): return lax.ppermute(array, axis, route)  28.3 us
    ppermute x14, waiting for transfers between devices, shifted(): return lax.ppermute(array, axis, route)  27.2 us
    ppermute x17, starting transfers between devices, exchanged(): lax.ppermute(array, axis, [(i, i ^ flip) for i in range(lax.axis_size(axi...  22.7 us
    ppermute x17, waiting for transfers between devices, exchanged(): lax.ppermute(array, axis, [(i, i ^ flip) for i in range(lax.axis_size(axi...  16.4 us
    pallas_call x18, Pallas kernels, on_chip(): pl.pallas_call(run, in_specs=[pl.BlockSpec(memory_space=pltpu.VMEM)] * co...  9.32 us
    unnamed x20, local copies, waits for them, and re-layouts  6.98 us
    dot_general x3, matrix products, dot(): return lax.dot_general(a, b, dims, preferred_element_type=F32)  5.86 us
  transfers between devices with their start and end apart: 31, of which 13 were waited for; matrix products, arithmetic and copies ran while one was open for 4% of the time, Pallas kernels for 20%

commit v1 on v0

--- a/solution.py
+++ b/solution.py
@@ -24,6 +24,7 @@
 MIB = 1024 * 1024
 FINISH_FLOPS = 6 * 10**9
 LANES = 128
+ATTENTION_MIB = 46
 
 NT = (((1,), (1,)), ((), ()))
 TN = (((0,), (0,)), ((), ()))
@@ -76,12 +77,13 @@
 
 
 def attention_kernel(band_rows, band_cols, total_rows, head_width, extra, first, count, *refs):
-    (start_ref, mask_ref, left_ref, right_ref, above_ref, below_ref, cl_ref, cr_ref,
+    (place_ref, mask_ref, left_ref, right_ref, rows_a, rows_b, corners_a, corners_b,
      qkv_hbm, grad_hbm, w_hbm) = refs[:11]
-    (dq_ref, top_ref, bottom_ref, mid_ref, to_left_ref, to_right_ref,
+    (dq_ref, out_a, out_b, mid_ref, to_left_ref, to_right_ref,
      halo_ref, spot_ref, q_ref, k_ref, v_ref, dk_ref, dv_ref,
      own_refs, w_refs, own_sem, w_sem) = refs[11 + extra :]
-    band_start = start_ref[0]
+    band_start = place_ref[0]
+    even = place_ref[1] == 0
     tiles = band_rows // TILE_R
     queries = TILE_R * band_cols
     keys = REGION_R * KEY_COLS
@@ -121,10 +123,12 @@
                 copy.start()
         halo_ref[:side] = left_ref[...]
         halo_ref[side:at_above] = right_ref[...]
-        halo_ref[at_above:at_below] = above_ref[...]
-        halo_ref[at_below:at_cl] = below_ref[...]
-        halo_ref[at_cl : at_cl + corner] = cl_ref[...]
-        halo_ref[at_cr : at_cr + corner] = cr_ref[...]
+        for above, below, size, refs_ab in (
+            (at_above, at_below, edge, (rows_a, rows_b)),
+            (at_cl, at_cr, corner, (corners_a, corners_b)),
+        ):
+            for ref, at in zip(refs_ab, (jnp.where(even, below, above), jnp.where(even, above, below))):
+                halo_ref[pl.ds(pl.multiple_of(at, 16), size), :] = ref[...]
         spot_ref[...] = jnp.zeros_like(spot_ref)
 
     def place(target, own, weights):
@@ -138,15 +142,12 @@
                 spot_ref[part, pl.ds(start + MARGIN, band_rows, stride=HALO_COLS), :] = fresh[
                     side + col * band_rows : side + (col + 1) * band_rows, at
                 ]
-        for corner_at, offset in ((at_cl, 0), (at_cr, MARGIN)):
-            for rim in range(2):
-                first = rim * (MARGIN + band_rows) * HALO_COLS + offset
-                for col in range(MARGIN):
-                    base = corner_at + (rim * MARGIN + col) * EDGE_R
-                    for part, at in halves:
-                        spot_ref[part, pl.ds(first + col, MARGIN, stride=HALO_COLS), :] = fresh[
-                            base : base + MARGIN, at
-                        ]
+        for corner_at, skip, row in ((at_cl, PAD_R, 0), (at_cr, 0, MARGIN + band_rows)):
+            for col in range(2 * MARGIN):
+                base = corner_at + col * EDGE_R + skip
+                spot = pl.ds(row * HALO_COLS + col, MARGIN, stride=HALO_COLS)
+                for part, at in halves:
+                    spot_ref[part, spot, :] = fresh[base : base + MARGIN, at]
         for row in range(region_rows):
             base = row * KEY_COLS
             inner = row - MARGIN
@@ -217,15 +218,18 @@
     below = (PAD_R + MARGIN + band_rows) * KEY_COLS
     for part, acc in enumerate((dk_ref, dv_ref)):
         for lane, at in halves:
-            for row in range(MARGIN):
-                here = slice(row * band_cols, (row + 1) * band_cols)
-                for start, out in ((PAD_R * KEY_COLS, top_ref), (below, bottom_ref)):
-                    start = start + row * KEY_COLS
-                    out[part, here, at] = acc[lane, start : start + band_cols, :].astype(BF)
-            for pair in range(MARGIN):
-                here = slice(edge + pair * 2 * EDGE_R, edge + (pair + 1) * 2 * EDGE_R)
-                for start, out in ((0, top_ref), (below, bottom_ref)):
-                    start = start + band_cols + 2 * pair
+            for out, own_at, side_at in (
+                (out_a, jnp.where(even, below, PAD_R * KEY_COLS), jnp.where(even, below, 0)),
+                (out_b, jnp.where(even, PAD_R * KEY_COLS, below), jnp.where(even, 0, below)),
+            ):
+                for row in range(MARGIN):
+                    start = pl.multiple_of(own_at + row * KEY_COLS, KEY_COLS)
+                    out[part, row * band_cols : (row + 1) * band_cols, at] = acc[
+                        lane, pl.ds(start, band_cols), :
+                    ].astype(BF)
+                for pair in range(MARGIN):
+                    here = slice(edge + pair * 2 * EDGE_R, edge + (pair + 1) * 2 * EDGE_R)
+                    start = side_at + band_cols + 2 * pair
                     out[part, here, at] = jnp.concatenate(
                         [
                             acc[lane, pl.ds(start, EDGE_R, stride=KEY_COLS), :],
@@ -303,7 +307,7 @@
             pltpu.SemaphoreType.DMA((count, 2)),
         ],
         compiler_params=pltpu.CompilerParams(
-            dimension_semantics=("arbitrary",), vmem_limit_bytes=30 * MIB
+            dimension_semantics=("arbitrary",), vmem_limit_bytes=ATTENTION_MIB * MIB
         ),
         cost_estimate=pl.CostEstimate(
             flops=count * 14 * 10**9, bytes_accessed=count * 8 * MIB, transcendentals=count * 10**6
@@ -311,22 +315,23 @@
     )(start, masks, *halo, qkv, grad_out, w_qkv, *[a for _, a in before], *after)
 
 
-def on_chip(kernel, out_shape, operands, after=(), scratch=(), flops=10**5):
-    count = len(operands)
+def on_chip(kernel, out_shape, operands, after=(), scratch=(), flops=10**5, place=()):
+    count = len(operands) + len(place)
 
     def run(*refs):
         kernel(*refs[:count], *refs[count + len(after) :])
 
     return pl.pallas_call(
         run,
-        in_specs=[pl.BlockSpec(memory_space=pltpu.VMEM)] * count
+        in_specs=[pl.BlockSpec(memory_space=pltpu.SMEM)] * len(place)
+        + [pl.BlockSpec(memory_space=pltpu.VMEM)] * len(operands)
         + [pl.BlockSpec(memory_space=pl.ANY)] * len(after),
         out_specs=[pl.BlockSpec(memory_space=pltpu.VMEM)] * len(out_shape),
         out_shape=[jax.ShapeDtypeStruct(s, d) for s, d in out_shape],
         scratch_shapes=list(scratch),
         compiler_params=pltpu.CompilerParams(vmem_limit_bytes=24 * MIB),
         cost_estimate=pl.CostEstimate(flops=flops, bytes_accessed=10**4, transcendentals=0),
-    )(*operands, *after)
+    )(*place, *operands, *after)
 
 
 def lanes_of(width):
@@ -351,7 +356,7 @@
         + [pl.BlockSpec(memory_space=pl.ANY)] * len(after),
         out_specs=pl.BlockSpec((tokens, block), lambda g: (0, g)),
         out_shape=jax.ShapeDtypeStruct((tokens, columns), BF),
-        compiler_params=pltpu.CompilerParams(vmem_limit_bytes=24 * MIB),
+        compiler_params=pltpu.CompilerParams(vmem_limit_bytes=56 * MIB),
         cost_estimate=pl.CostEstimate(flops=10**9, bytes_accessed=MIB, transcendentals=0),
     )(own, w_qkv, *after)
 
@@ -366,7 +371,7 @@
         out_refs, wide_ref = refs[len(after) : -1], refs[-1]
         for at in range(0, width, 2 * LANES):
             wide_ref[at : at + 2 * LANES, :] = own_ref[:, at : at + 2 * LANES].astype(F32).T
-        me = me_ref[0]
+        me = me_ref[2]
         for i, order in enumerate(orders):
             for j in range(0, devices, step):
                 rows = [
@@ -409,44 +414,50 @@
     return on_chip(kernel, [out, out], [own], scratch=scratch)
 
 
-def pack_rows(own, band_cols, after):
+def pack_rows(place, own, band_cols, after):
     tokens, width = own.shape
     edge = MARGIN * band_cols
 
-    def kernel(own_ref, last_ref, first_ref):
-        last_ref[...] = own_ref[tokens - edge :, :]
-        first_ref[...] = own_ref[:edge, :]
+    def kernel(place_ref, own_ref, out_a, out_b):
+        even = place_ref[1] == 0
+        last, first = own_ref[tokens - edge :, :], own_ref[:edge, :]
+        out_a[...] = jnp.where(even, last, first)
+        out_b[...] = jnp.where(even, first, last)
 
     out = ((edge, width), BF)
-    return on_chip(kernel, [out, out], [own], after=after)
-
-
-def pack_corners(above, below, band_cols):
-    edge, width = above.shape
-
-    def kernel(above_ref, below_ref, last_ref, first_ref, wide_ref):
-        wide_ref[:, edge:, :] = jnp.zeros_like(wide_ref[:, edge:, :])
-        for rim, rim_ref in enumerate((above_ref, below_ref)):
-            for lane, at in lanes_of(width):
-                wide_ref[lane, :edge, :] = rim_ref[:, at].astype(F32)
-                for out_ref, offset in ((last_ref, band_cols - MARGIN), (first_ref, 0)):
-                    for col in range(0, MARGIN, 2):
-                        base = (rim * MARGIN + col) * EDGE_R
-                        pair = [
-                            wide_ref[lane, pl.ds(offset + c, EDGE_R, stride=band_cols), :]
-                            for c in (col, col + 1)
+    return on_chip(kernel, [out, out], [own], after=after, place=[place])
+
+
+def pack_corners(place, left, right, band_rows, after):
+    width = left.shape[1]
+
+    def kernel(place_ref, left_ref, right_ref, out_a, out_b):
+        even = place_ref[1] == 0
+        for side, side_ref in enumerate((left_ref, right_ref)):
+            for col in range(0, MARGIN, 2):
+                base = (side * MARGIN + col) * EDGE_R
+                last, first = (
+                    jnp.concatenate(
+                        [
+                            side_ref[at : at + EDGE_R, :].astype(F32)
+                            for at in (start, start + band_rows)
                         ]
-                        out_ref[base : base + 2 * EDGE_R, at] = jnp.concatenate(pair).astype(BF)
+                    )
+                    for start in ((col + 1) * band_rows - EDGE_R, col * band_rows)
+                )
+                here = slice(base, base + 2 * EDGE_R)
+                out_a[here, :] = jnp.where(even, last, first).astype(BF)
+                out_b[here, :] = jnp.where(even, first, last).astype(BF)
 
     out = ((2 * MARGIN * EDGE_R, width), BF)
-    scratch = [pltpu.VMEM((width // LANES, EDGE_R * band_cols, LANES), F32)]
-    return on_chip(kernel, [out, out], [above, below], scratch=scratch)
-
-
-def merge_sides(left, right, above, below, band_rows, band_cols, after=()):
+    return on_chip(kernel, [out, out], [left, right], after=after, place=[place])
+
+
+def merge_sides(place, left, right, rim_a, rim_b, band_rows, band_cols, after=()):
     edge = MARGIN * band_cols
 
-    def kernel(left_ref, right_ref, above_ref, below_ref, ol_ref, or_ref):
+    def kernel(place_ref, left_ref, right_ref, a_ref, b_ref, ol_ref, or_ref):
+        even = place_ref[1] == 0
         for part in range(2):
             for col in range(2 * MARGIN):
                 source, target = (left_ref, ol_ref) if col < MARGIN else (right_ref, or_ref)
@@ -454,28 +465,31 @@
                 pair = slice(edge + (col // 2) * 2 * EDGE_R, edge + (col // 2 + 1) * 2 * EDGE_R)
                 odd = slice((col % 2) * EDGE_R, (col % 2 + 1) * EDGE_R)
                 rows = source[part, base : base + band_rows, :].astype(F32)
-                first = rows[:EDGE_R] + above_ref[part, pair, :].astype(F32)[odd]
-                last = rows[band_rows - EDGE_R :] + below_ref[part, pair, :].astype(F32)[odd]
+                rim_a, rim_b = (ref[part, pair, :].astype(F32)[odd] for ref in (a_ref, b_ref))
+                first = rows[:EDGE_R] + jnp.where(even, rim_b, rim_a)
+                last = rows[band_rows - EDGE_R :] + jnp.where(even, rim_a, rim_b)
                 target[part, base : base + band_rows, :] = jnp.concatenate(
                     [first, rows[EDGE_R : band_rows - EDGE_R], last], axis=0
                 ).astype(BF)
 
     out = [(left.shape, BF), (right.shape, BF)]
-    return on_chip(kernel, out, [left, right, above, below], after=after)
-
-
-def finish(mid, above, below, left, right, band_rows, band_cols, after, flops):
+    return on_chip(kernel, out, [left, right, rim_a, rim_b], after=after, place=[place])
+
+
+def finish(place, mid, rim_a, rim_b, left, right, band_rows, band_cols, after, flops):
     _, tokens, width = mid.shape
     edge = MARGIN * band_cols
 
-    def kernel(mid_ref, above_ref, below_ref, left_ref, right_ref, out_ref, acc_ref):
+    def kernel(place_ref, mid_ref, a_ref, b_ref, left_ref, right_ref, out_ref, acc_ref):
+        even = place_ref[1] == 0
         for part in range(2):
             for block in range(width // (2 * LANES)):
                 for lane in range(2):
                     at = slice((2 * block + lane) * LANES, (2 * block + lane + 1) * LANES)
                     acc_ref[lane] = mid_ref[part, :, at].astype(F32)
-                    acc_ref[lane, :edge, :] += above_ref[part, :edge, at].astype(F32)
-                    acc_ref[lane, tokens - edge :, :] += below_ref[part, :edge, at].astype(F32)
+                    from_a, from_b = (r[part, :edge, at].astype(F32) for r in (a_ref, b_ref))
+                    acc_ref[lane, :edge, :] += jnp.where(even, from_b, from_a)
+                    acc_ref[lane, tokens - edge :, :] += jnp.where(even, from_a, from_b)
                     for col in range(MARGIN):
                         here = slice(col * band_rows, (col + 1) * band_rows)
                         first = pl.ds(col, band_rows, stride=band_cols)
@@ -488,8 +502,8 @@
 
     out = [((tokens, 2 * width), BF)]
     scratch = [pltpu.VMEM((2, tokens, LANES), F32)]
-    operands = [mid, above, below, left, right]
-    return on_chip(kernel, out, operands, after, scratch, flops)[0]
+    operands = [mid, rim_a, rim_b, left, right]
+    return on_chip(kernel, out, operands, after, scratch, flops, [place])[0]
 
 
 def grad_rows(rows, columns, scale, kind, after=()):
@@ -567,6 +581,16 @@
     return lax.ppermute(array, axis, route)
 
 
+def swapped(array_a, array_b, axis):
+    size = lax.axis_size(axis)
+    pairs = [(i, i + 1) for i in range(size - 1)]
+    route = lambda chosen: chosen + [(j, i) for i, j in chosen]
+    return [
+        lax.ppermute(array, axis, route(pairs[offset::2]))
+        for array, offset in ((array_a, 0), (array_b, 1))
+    ]
+
+
 def exchanged(array, axis, flip):
     return lax.ppermute(array, axis, [(i, i ^ flip) for i in range(lax.axis_size(axis))])
 
@@ -598,60 +622,53 @@
     last_cols, first_cols = pack_sides(own, band_rows, band_cols)
     left = shifted(last_cols, "lon", 1, True)
     right = shifted(first_cols, "lon", -1, True)
-    last_rows, first_rows = pack_rows(own, band_cols, [last_cols])
-    above = shifted(last_rows, "lat", 1, False)
-    below = shifted(first_rows, "lat", -1, False)
-    last_corners, first_corners = pack_corners(above, below, band_cols)
-    corner_left = shifted(last_corners, "lon", 1, True)
-    corner_right = shifted(first_corners, "lon", -1, True)
-    halo = (left, right, above, below, corner_left, corner_right)
-
-    start = band_start.reshape(1)
+    me = (lax.axis_index("dp") * n_lat + lax.axis_index("lat")) * n_lon + lax.axis_index("lon")
+    start = jnp.stack([band_start, lax.axis_index("lat") % 2, me])
+    rim_rows = swapped(*pack_rows(start, own, band_cols, [last_cols]), "lat")
+
     masks = window_masks(start, band_rows, band_cols, total_rows)
-    qkv = project(own, w_qkv, [last_corners])
+    qkv = project(own, w_qkv, [last_cols])
     lat_bits = bits_of("lat")
     x_first = lat_bits[:1] + bits_of("dp") + lat_bits[1:]
     y_first = lat_bits + bits_of("dp")
-    me = (lax.axis_index("dp") * n_lat + lax.axis_index("lat")) * n_lon + lax.axis_index("lon")
     half = width // 2
     rows_x, rows_y = row_blocks(
-        me.reshape(1), own, [feature_order(x_first), feature_order(y_first)], [last_corners]
+        start, own, [feature_order(x_first), feature_order(y_first)], [last_cols]
     )
+    corners = pack_corners(start, left, right, band_rows, [masks, qkv, *rows_x, *rows_y])
+    halo = (left, right, *rim_rows, *swapped(*corners, "lat"))
     scale = float(tokens * n_dp * n_lat * n_lon) ** -0.5
 
     attend = lambda first, count, before, after: attention_grads(
         first, count, slots, start, masks, halo, qkv, flat_grad, w_qkv, shape, before, after
     )
 
-    def return_rows(grads):
-        from_below = shifted(grads[1], "lat", -1, False)
-        from_above = shifted(grads[2], "lat", 1, False)
-        return from_above, from_below
-
     def return_sides(grads, rims, after):
-        to_left, to_right = merge_sides(grads[4], grads[5], *rims, band_rows, band_cols, after)
+        to_left, to_right = merge_sides(
+            start, grads[4], grads[5], *rims, band_rows, band_cols, after
+        )
         from_right = shifted(to_left, "lon", -1, True)
         from_left = shifted(to_right, "lon", 1, True)
         return to_left, from_left, from_right
 
     one = attend(0, slots, [], [*rows_x, *rows_y])
-    rims_1 = return_rows(one)
+    rims_1 = swapped(one[1], one[2], "lat")
     two = attend(slots, 1, [(0, one[0])], [])
     sent, *sides_1 = return_sides(one, rims_1, [two[1]])
     two = attend(slots + 1, 1, list(enumerate(two)), [sent])
-    rims_2 = return_rows(two)
+    rims_2 = swapped(two[1], two[2], "lat")
     dq = two[0]
 
     send_q = grad_rows([rows_x[1]], dq, scale, BF, after=sides_1)
     keep_q = dot(rows_x[0], dq) * scale
     sent, *sides_2 = return_sides(two, rims_2, [send_q])
-    dkv_1 = finish(one[3], *rims_1, *sides_1, band_rows, band_cols, [sent], 10**5)
+    dkv_1 = finish(start, one[3], *rims_1, *sides_1, band_rows, band_cols, [sent], 10**5)
     send_1 = grad_rows([rows_y[1]], dkv_1, scale, BF)
     keep_1 = dot(rows_y[0], dkv_1) * scale
     received = [exchanged(send_q, *x_first[0]), exchanged(send_1, *y_first[0])]
     keep, send = add_split(jnp.concatenate([keep_q, keep_1], axis=1), received)
 
-    dkv_2 = finish(two[3], *rims_2, *sides_2, band_rows, band_cols, [keep], FINISH_FLOPS)
+    dkv_2 = finish(start, two[3], *rims_2, *sides_2, band_rows, band_cols, [keep], FINISH_FLOPS)
     for step_x, step_y in zip(x_first[1:-1], y_first[1:-1]):
         received = [exchanged(send[0], *step_x), exchanged(send[1], *step_y)]
         keep, send = add_split(keep, received, [dkv_2])

time: 164 us -> 158 us (0.963)
  waiting for transfers between devices: 43.6 us -> 31.4 us
  Pallas kernels: 54.2 us -> 64.1 us
  local copies, waits for them, and re-layouts: 7.02 us -> 5.27 us
    ppermute x14 -> x6, starting transfers between devices: 28.3 us -> 11.1 us  [shifted(): return lax.ppermute(array, axis, route)]
    ppermute x0 -> x8, starting transfers between devices: none -> 12.9 us  [swapped(): lax.ppermute(array, axis, route(pairs[offset::2]))]
    ppermute x14 -> x6, waiting for transfers between devices: 27.2 us -> 16.8 us  [shifted(): return lax.ppermute(array, axis, route)]
    pallas_call x1, Pallas kernels: 4.88 us -> 8.37 us  [project(): pl.pallas_call(kernel, grid=(columns // block,), in_specs=[pl.BlockSpec((...]
    pallas_call x3, Pallas kernels: 36.1 us -> 38.8 us  [attention_grads(): pl.pallas_call(functools.partial(attention_kernel, band_rows, band_cols,...]
    ppermute x17, starting transfers between devices: 22.7 us -> 25.4 us  [exchanged(): lax.ppermute(array, axis, [(i, i ^ flip) for i in range(lax.axis_size(axi...]
    pallas_call x18, Pallas kernels: 9.32 us -> 11.8 us  [on_chip(): pl.pallas_call(run, in_specs=[pl.BlockSpec(memory_space=pltpu.SMEM)] * le...]
    ppermute x17, waiting for transfers between devices: 16.4 us -> 14.2 us  [exchanged(): lax.ppermute(array, axis, [(i, i ^ flip) for i in range(lax.axis_size(axi...]
  transfers between devices with their start and end apart: 31 -> 31, of which waited for: 13 -> 9; matrix products, arithmetic and copies ran while one was open for 4% -> 4% of each run, Pallas kernels for 20% -> 25%
where the time goes in v1:
time: 158 us
  Pallas kernels  64.1 us (41%)
  starting transfers between devices  49.4 us (31%)
  waiting for transfers between devices  31.4 us (20%)
  matrix products  5.86 us (4%)
  local copies, waits for them, and re-layouts  5.27 us (3%)
    pallas_call x3, Pallas kernels, attention_grads(): pl.pallas_call(functools.partial(attention_kernel, band_rows, band_cols,...  38.8 us
    ppermute x17, starting transfers between devices, exchanged(): lax.ppermute(array, axis, [(i, i ^ flip) for i in range(lax.axis_size(axi...  25.4 us
    ppermute x6, waiting for transfers between devices, shifted(): return lax.ppermute(array, axis, route)  16.8 us
    ppermute x17, waiting for transfers between devices, exchanged(): lax.ppermute(array, axis, [(i, i ^ flip) for i in range(lax.axis_size(axi...  14.2 us
    ppermute x8, starting transfers between devices, swapped(): lax.ppermute(array, axis, route(pairs[offset::2]))  12.9 us
    pallas_call x18, Pallas kernels, on_chip(): pl.pallas_call(run, in_specs=[pl.BlockSpec(memory_space=pltpu.SMEM)] * le...  11.8 us
    ppermute x6, starting transfers between devices, shifted(): return lax.ppermute(array, axis, route)  11.1 us
    pallas_call x1, Pallas kernels, project(): pl.pallas_call(kernel, grid=(columns // block,), in_specs=[pl.BlockSpec((...  8.37 us
  transfers between devices with their start and end apart: 31, of which 9 were waited for; matrix products, arithmetic and copies ran while one was open for 4% of the time, Pallas kernels for 25%

profile of v1, /device:TPU:0, one launch (start us, length us, event | category | flops | bytes accessed | tf_op | source)
XLA Modules:
  0.0 157.6 jit_solution(11660462828054487514)
XLA Ops:
  2.6 5.1 %collective-permute-start.1 = (bf16[192,1024]{1,0:T(8,128)(2,1)S(1)}, bf16[192,1024]{1,0:T(8,128)(2,1)S(1)}, u32[]{:S(2)}, u32[]{:S(2)}) collective-permute-start(bf16[192,1024]{1,0:T(8,128)(2,1)S(1)} %get-tuple-element.55), channel_id=1, source_target_pairs={{0,3},{1,0},{2,1},{3,2},{4,7},{5,4},{6,5},{7,6},{8,11},{9,8},{10,9... | collective-permute-start | bytes 1179656 | tf_op jit(solution)/shard_map/ppermute | solution.py:581
  10.4 4.0 %shard_map.50.refs_3_.refs_1_ = bf16[8,512,128]{2,1,0:T(8,128)(2,1)} custom-call(s32[3]{0:T(128)} %copy-done.7), custom_call_target="tpu_custom_call" | custom-call | flops 10000000 | bytes 2097152 | tf_op jit(solution)/shard_map/pallas_call | solution.py:69
  16.2 8.4 %shard_map.53.refs_4_.refs_8_ = bf16[512,3072]{1,0:T(8,128)(2,1)} custom-call(bf16[512,1024]{1,0:T(8,128)(2,1)} %bitcast.12, bf16[1024,3072]{1,0:T(8,128)(2,1)} %refs_10_.5, bf16[192,1024]{1,0:T(8,128)(2,1)} %copy-done.6), custom_call_target="tpu_custom_call" | custom-call | flops 1000000000 | bytes 1048576 | tf_op jit(solution)/shard_map/pallas_call | solution.py:349
  25.5 1.9 %copy-done = bf16[512,3072]{1,0:T(8,128)(2,1)S(1)} copy-done((bf16[512,3072]{1,0:T(8,128)(2,1)S(1)}, bf16[512,3072]{1,0:T(8,128)(2,1)}, u32[]{:S(2)}) %copy-start) | copy-done | bytes 3145752
  28.0 2.1 %collective-permute-start.4 = (bf16[96,1024]{1,0:T(8,128)(2,1)S(1)}, bf16[96,1024]{1,0:T(8,128)(2,1)S(1)}, u32[]{:S(2)}, u32[]{:S(2)}) collective-permute-start(bf16[96,1024]{1,0:T(8,128)(2,1)S(1)} %get-tuple-element.62), channel_id=1, source_target_pairs={{0,4},{8,12},{4,0},{12,8},{1,5},{9,13},{5,1},{13,9},{2,6},{10,14},... | collective-permute-start | bytes 589832 | tf_op jit(solution)/shard_map/ppermute | solution.py:589
  31.2 19.0 %shard_map.56 = (bf16[512,1024]{1,0:T(8,128)(2,1)S(1)}, bf16[2,192,512]{2,1,0:T(8,128)(2,1)S(1)}, bf16[2,192,512]{2,1,0:T(8,128)(2,1)S(1)}, bf16[2,512,512]{2,1,...) custom-call(s32[3]{0:T(128)S(1)} %copy-done.9, ...), custom_call_target="tpu_custom_call" | custom-call | flops 28000000000 | bytes 16777216 | tf_op jit(solution)/shard_map/pallas_call | solution.py:279
  50.1 6.0 %collective-permute-start.6 = (bf16[2,192,512]{2,1,0:T(8,128)(2,1)S(1)}, bf16[2,192,512]{2,1,0:T(8,128)(2,1)S(1)}, u32[]{:S(2)}, u32[]{:S(2)}) collective-permute-start(bf16[2,192,512]{2,1,0:T(8,128)(2,1)S(1)} %get-tuple-element.73), channel_id=1, source_target_pairs={{0,4},{8,12},{4,0},{12,8},{1,5},{9,13},{5,1},{13,9},{2,6},{10,14},... | collective-permute-start | bytes 1179656 | tf_op jit(solution)/shard_map/ppermute | solution.py:589
  57.0 9.9 %shard_map.57 = (bf16[512,1024]{1,0:T(8,128)(2,1)S(1)}, bf16[2,192,512]{2,1,0:T(8,128)(2,1)S(1)}, bf16[2,192,512]{2,1,0:T(8,128)(2,1)S(1)}, bf16[2,512,512]{2,1,...) custom-call(s32[3]{0:T(128)S(1)} %copy-done.9, ...), custom_call_target="tpu_custom_call", output_to_operand_aliasing={{0}: (11, {})} | custom-call | flops 14000000000 | bytes 8388608 | tf_op jit(solution)/shard_map/pallas_call | solution.py:279
  67.7 3.9 %collective-permute-start.9 = (bf16[2,192,512]{2,1,0:T(8,128)(2,1)S(1)}, bf16[2,192,512]{2,1,0:T(8,128)(2,1)S(1)}, u32[]{:S(2)}, u32[]{:S(2)}) collective-permute-start(bf16[2,192,512]{2,1,0:T(8,128)(2,1)S(1)} %get-tuple-element.75.refs_17_), channel_id=1, source_target_pairs={{0,3},{1,0},{2,1},{3,2},{4,7},{5,4},{6,5},{7,6},{8,11},{9,8},{10,9... | collective-permute-start | bytes 1179656 | tf_op jit(solution)/shard_map/ppermute | solution.py:581
  71.6 9.9 %shard_map.59 = (bf16[512,1024]{1,0:T(8,128)(2,1)S(1)}, bf16[2,192,512]{2,1,0:T(8,128)(2,1)S(1)}, bf16[2,192,512]{2,1,0:T(8,128)(2,1)S(1)}, bf16[2,512,512]{2,1,...) custom-call(s32[3]{0:T(128)S(1)} %copy-done.9, ...), custom_call_target="tpu_custom_call", output_to_operand_aliasing={{0}: (11, {}), {1}: (12, {}), {2}: (13, {}), {3}: (14, {}),... | custom-call | flops 14000000000 | bytes 8388608 | tf_op jit(solution)/shard_map/pallas_call | solution.py:279
  84.1 2.9 %collective-permute-done.9.refs_3_.refs_5_ = bf16[2,192,512]{2,1,0:T(8,128)(2,1)S(1)} collective-permute-done((bf16[2,192,512]{2,1,0:T(8,128)(2,1)S(1)}, bf16[2,192,512]{2,1,0:T(8,128)(2,1)S(1)}, u32[]{:S(2)}, u32[]{:S(2)}) %collective-permute-start.9) | collective-permute-done | bytes 393248 | tf_op jit(solution)/shard_map/ppermute | solution.py:581
  88.4 1.9 %shard_map.62.refs_1_ = bf16[512,1024]{1,0:T(8,128)(2,1)S(1)} custom-call(s32[3]{0:T(128)S(1)} %copy-done.9, bf16[2,512,512]{2,1,0:T(8,128)(2,1)S(1)} %get-tuple-element.77.refs_1_, bf16[2,192,512]{2,1,0:T(8,128)(2,1)S(1)} %collective-permute-done.6.refs_3_.refs_2_, bf16[2,192,512]{2,1,0:T(8,128)(2,1)S(1)} %collective-permute-done.7.refs_4_.refs_3_, ...), custom_call_target="tpu_custom_call" | custom-call | flops 100000 | bytes 10000 | tf_op jit(solution)/shard_map/pallas_call | solution.py:324
  91.1 4.6 %collective-permute-start.15 = (bf16[512,1024]{1,0:T(8,128)(2,1)S(1)}, bf16[512,1024]{1,0:T(8,128)(2,1)S(1)}, u32[]{:S(2)}, u32[]{:S(2)}) collective-permute-start(bf16[512,1024]{1,0:T(8,128)(2,1)S(1)} %shard_map.63), channel_id=1, source_target_pairs={{0,4},{4,0},{8,12},{12,8},{1,5},{5,1},{9,13},{13,9},{2,6},{6,2},{1... | collective-permute-start | bytes 3145736 | tf_op jit(solution)/shard_map/ppermute | solution.py:595
  101.7 1.7 %collective-permute-start.17 = (bf16[256,1024]{1,0:T(8,128)(2,1)S(1)}, bf16[256,1024]{1,0:T(8,128)(2,1)S(1)}, u32[]{:S(2)}, u32[]{:S(2)}) collective-permute-start(bf16[256,1024]{1,0:T(8,128)(2,1)S(1)} %get-tuple-element.88), channel_id=1, source_target_pairs={{0,8},{4,12},{8,0},{12,4},{1,9},{5,13},{9,1},{13,5},{2,10},{6,14},... | collective-permute-start | bytes 1572872 | tf_op jit(solution)/shard_map/ppermute | solution.py:595
  103.4 13.0 %collective-permute-done.12.refs_4_ = bf16[2,192,512]{2,1,0:T(8,128)(2,1)S(1)} collective-permute-done((bf16[2,192,512]{2,1,0:T(8,128)(2,1)S(1)}, bf16[2,192,512]{2,1,0:T(8,128)(2,1)S(1)}, u32[]{:S(2)}, u32[]{:S(2)}) %collective-permute-start.12) | collective-permute-done | bytes 393248 | tf_op jit(solution)/shard_map/ppermute | solution.py:581
  116.4 1.9 %shard_map.65.refs_3_.refs_2_ = bf16[512,1024]{1,0:T(8,128)(2,1)S(1)} custom-call(s32[3]{0:T(128)S(1)} %copy-done.9, bf16[2,512,512]{2,1,0:T(8,128)(2,1)S(1)} %get-tuple-element.84.refs_1_, bf16[2,192,512]{2,1,0:T(8,128)(2,1)S(1)} %collective-permute-done.10.refs_3_.refs_2_, bf16[2,192,512]{2,1,0:T(8,128)(2,1)S(1)} %collective-permute-done.11.refs_4_.refs_3_, ...), custom_call_target="tpu_custom_call" | custom-call | flops 6000000000 | bytes 10000 | tf_op jit(solution)/shard_map/pallas_call | solution.py:324
  125.5 4.0 %collective-permute-done.18.refs_1_ = bf16[128,1024]{1,0:T(8,128)(2,1)S(1)} collective-permute-done((bf16[128,1024]{1,0:T(8,128)(2,1)S(1)}, bf16[128,1024]{1,0:T(8,128)(2,1)S(1)}, u32[]{:S(2)}, u32[]{:S(2)}) %collective-permute-start.18) | collective-permute-done | bytes 262176 | tf_op jit(solution)/shard_map/ppermute | solution.py:595
  131.2 1.9 %collective-permute-start.20 = (bf16[32,2048]{1,0:T(8,128)(2,1)S(1)}, bf16[32,2048]{1,0:T(8,128)(2,1)S(1)}, u32[]{:S(2)}, u32[]{:S(2)}) collective-permute-start(bf16[32,2048]{1,0:T(8,128)(2,1)S(1)} %get-tuple-element.93), channel_id=1, source_target_pairs={{0,1},{1,0},{2,3},{3,2},{4,5},{5,4},{6,7},{7,6},{8,9},{9,8},{10,11... | collective-permute-start | bytes 393224 | tf_op jit(solution)/shard_map/ppermute | solution.py:595
  133.0 3.0 %collective-permute-done.24.refs_1_ = bf16[256,512]{1,0:T(8,128)(2,1)S(1)} collective-permute-done((bf16[256,512]{1,0:T(8,128)(2,1)S(1)}, bf16[256,512]{1,0:T(8,128)(2,1)S(1)}, u32[]{:S(2)}, u32[]{:S(2)}) %collective-permute-start.24) | collective-permute-done | bytes 262176 | tf_op jit(solution)/shard_map/ppermute | solution.py:595
  139.6 2.6 %collective-permute-start.22 = (bf16[32,2048]{1,0:T(8,128)(2,1)S(1)}, bf16[32,2048]{1,0:T(8,128)(2,1)S(1)}, u32[]{:S(2)}, u32[]{:S(2)}) collective-permute-start(bf16[32,2048]{1,0:T(8,128)(2,1)S(1)} %get-tuple-element.95), channel_id=1, source_target_pairs={{0,3},{1,2},{2,1},{3,0},{4,7},{5,6},{6,5},{7,4},{8,11},{9,10},{10,... | collective-permute-start | bytes 393224 | tf_op jit(solution)/shard_map/ppermute | solution.py:595
  144.1 2.6 %collective-permute-start.30 = (bf16[32,1024]{1,0:T(8,128)(2,1)S(1)}, bf16[32,1024]{1,0:T(8,128)(2,1)S(1)}, u32[]{:S(2)}, u32[]{:S(2)}) collective-permute-start(bf16[32,1024]{1,0:T(8,128)(2,1)S(1)} %get-tuple-element.105), channel_id=1, source_target_pairs={{0,3},{1,2},{2,1},{3,0},{4,7},{5,6},{6,5},{7,4},{8,11},{9,10},{10,... | collective-permute-start | bytes 196616 | tf_op jit(solution)/shard_map/ppermute | solution.py:595
  146.8 4.4 %convolution_convert_fusion = bf16[512,1024]{1,0:T(8,128)(2,1)} fusion(bf16[512,3072]{1,0:T(8,128)(2,1)S(1)} %slice_dynamic-update-slice_fusion, bf16[1024,3072]{1,0:T(8,128)(2,1)S(1)} %bitcast.20), kind=kOutput, calls=%fused_computation.3 | convolution fusion | flops 3221749760 | bytes 10485760 | tf_op jit(solution)/shard_map/dot_general | solution.py:35
  151.2 2.1 %collective-permute-done.21.refs_2_ = bf16[32,2048]{1,0:T(8,128)(2,1)S(1)} collective-permute-done((bf16[32,2048]{1,0:T(8,128)(2,1)S(1)}, bf16[32,2048]{1,0:T(8,128)(2,1)S(1)}, u32[]{:S(2)}, u32[]{:S(2)}) %collective-permute-start.21) | collective-permute-done | bytes 131104 | tf_op jit(solution)/shard_map/ppermute | solution.py:595
  153.3 3.5 %collective-permute-done.29.refs_6_ = bf16[32,1024]{1,0:T(8,128)(2,1)S(1)} collective-permute-done((bf16[32,1024]{1,0:T(8,128)(2,1)S(1)}, bf16[32,1024]{1,0:T(8,128)(2,1)S(1)}, u32[]{:S(2)}, u32[]{:S(2)}) %collective-permute-start.29) | collective-permute-done | bytes 65568 | tf_op jit(solution)/shard_map/ppermute | solution.py:595
  (99 shorter events, 36.3 us)
Async XLA Ops:
  2.6 22.0 %collective-permute-start.1 = (bf16[192,1024]{1,0:T(8,128)(2,1)S(1)}, bf16[192,1024]{1,0:T(8,128)(2,1)S(1)}, u32[]{:S(2)}, u32[]{:S(2)}) collective-permute-start(bf16[192,1024]{1,0:T(8,128)(2,1)S(1)} %get-tuple-element.55), channel_id=1, source_target_pairs={{0,3},{1,0},{2,1},{3,2},{4,7},{5,4},{6,5},{7,6},{8,11},{9,8},{10,9... | collective-permute-start | bytes 1179656 | tf_op jit(solution)/shard_map/ppermute | solution.py:581
  7.7 17.7 %collective-permute-start = (bf16[192,1024]{1,0:T(8,128)(2,1)S(1)}, bf16[192,1024]{1,0:T(8,128)(2,1)S(1)}, u32[]{:S(2)}, u32[]{:S(2)}) collective-permute-start(bf16[192,1024]{1,0:T(8,128)(2,1)S(1)} %get-tuple-element.54.refs_2_.refs_0_), channel_id=1, source_target_pairs={{0,1},{1,2},{2,3},{3,0},{4,5},{5,6},{6,7},{7,4},{8,9},{9,10},{10,1... | collective-permute-start | bytes 1179656 | tf_op jit(solution)/shard_map/ppermute | solution.py:581
  9.6 21.1 %collective-permute-start.2 = (bf16[96,1024]{1,0:T(8,128)(2,1)S(1)}, bf16[96,1024]{1,0:T(8,128)(2,1)S(1)}, u32[]{:S(2)}, u32[]{:S(2)}) collective-permute-start(bf16[96,1024]{1,0:T(8,128)(2,1)S(1)} %get-tuple-element.56), channel_id=1, source_target_pairs={{0,4},{8,12},{4,0},{12,8},{1,5},{9,13},{5,1},{13,9},{2,6},{10,14},... | collective-permute-start | bytes 589832 | tf_op jit(solution)/shard_map/ppermute | solution.py:589
  9.7 21.1 %collective-permute-start.3 = (bf16[96,1024]{1,0:T(8,128)(2,1)S(1)}, bf16[96,1024]{1,0:T(8,128)(2,1)S(1)}, u32[]{:S(2)}, u32[]{:S(2)}) collective-permute-start(bf16[96,1024]{1,0:T(8,128)(2,1)S(1)} %get-tuple-element.57), channel_id=1, source_target_pairs={{4,8},{8,4},{5,9},{9,5},{6,10},{10,6},{7,11},{11,7},{20,24},{24,20... | collective-permute-start | bytes 589832 | tf_op jit(solution)/shard_map/ppermute | solution.py:589
  50.1 16.8 %collective-permute-start.6 = (bf16[2,192,512]{2,1,0:T(8,128)(2,1)S(1)}, bf16[2,192,512]{2,1,0:T(8,128)(2,1)S(1)}, u32[]{:S(2)}, u32[]{:S(2)}) collective-permute-start(bf16[2,192,512]{2,1,0:T(8,128)(2,1)S(1)} %get-tuple-element.73), channel_id=1, source_target_pairs={{0,4},{8,12},{4,0},{12,8},{1,5},{9,13},{5,1},{13,9},{2,6},{10,14},... | collective-permute-start | bytes 1179656 | tf_op jit(solution)/shard_map/ppermute | solution.py:589
  56.1 10.8 %collective-permute-start.7 = (bf16[2,192,512]{2,1,0:T(8,128)(2,1)S(1)}, bf16[2,192,512]{2,1,0:T(8,128)(2,1)S(1)}, u32[]{:S(2)}, u32[]{:S(2)}) collective-permute-start(bf16[2,192,512]{2,1,0:T(8,128)(2,1)S(1)} %get-tuple-element.74), channel_id=1, source_target_pairs={{4,8},{8,4},{5,9},{9,5},{6,10},{10,6},{7,11},{11,7},{20,24},{24,20... | collective-permute-start | bytes 1179656 | tf_op jit(solution)/shard_map/ppermute | solution.py:589
  67.6 16.4 %collective-permute-start.8 = (bf16[2,192,512]{2,1,0:T(8,128)(2,1)S(1)}, bf16[2,192,512]{2,1,0:T(8,128)(2,1)S(1)}, u32[]{:S(2)}, u32[]{:S(2)}) collective-permute-start(bf16[2,192,512]{2,1,0:T(8,128)(2,1)S(1)} %get-tuple-element.78), channel_id=1, source_target_pairs={{0,1},{1,2},{2,3},{3,0},{4,5},{5,6},{6,7},{7,4},{8,9},{9,10},{10,1... | collective-permute-start | bytes 1179656 | tf_op jit(solution)/shard_map/ppermute | solution.py:581
  67.7 19.3 %collective-permute-start.9 = (bf16[2,192,512]{2,1,0:T(8,128)(2,1)S(1)}, bf16[2,192,512]{2,1,0:T(8,128)(2,1)S(1)}, u32[]{:S(2)}, u32[]{:S(2)}) collective-permute-start(bf16[2,192,512]{2,1,0:T(8,128)(2,1)S(1)} %get-tuple-element.75.refs_17_), channel_id=1, source_target_pairs={{0,3},{1,0},{2,1},{3,2},{4,7},{5,4},{6,5},{7,6},{8,11},{9,8},{10,9... | collective-permute-start | bytes 1179656 | tf_op jit(solution)/shard_map/ppermute | solution.py:581
  81.5 6.2 %collective-permute-start.10 = (bf16[2,192,512]{2,1,0:T(8,128)(2,1)S(1)}, bf16[2,192,512]{2,1,0:T(8,128)(2,1)S(1)}, u32[]{:S(2)}, u32[]{:S(2)}) collective-permute-start(bf16[2,192,512]{2,1,0:T(8,128)(2,1)S(1)} %get-tuple-element.81), channel_id=1, source_target_pairs={{0,4},{8,12},{4,0},{12,8},{1,5},{9,13},{5,1},{13,9},{2,6},{10,14},... | collective-permute-start | bytes 1179656 | tf_op jit(solution)/shard_map/ppermute | solution.py:589
  91.1 8.7 %collective-permute-start.15 = (bf16[512,1024]{1,0:T(8,128)(2,1)S(1)}, bf16[512,1024]{1,0:T(8,128)(2,1)S(1)}, u32[]{:S(2)}, u32[]{:S(2)}) collective-permute-start(bf16[512,1024]{1,0:T(8,128)(2,1)S(1)} %shard_map.63), channel_id=1, source_target_pairs={{0,4},{4,0},{8,12},{12,8},{1,5},{5,1},{9,13},{13,9},{2,6},{6,2},{1... | collective-permute-start | bytes 3145736 | tf_op jit(solution)/shard_map/ppermute | solution.py:595
  96.5 19.9 %collective-permute-start.13 = (bf16[2,192,512]{2,1,0:T(8,128)(2,1)S(1)}, bf16[2,192,512]{2,1,0:T(8,128)(2,1)S(1)}, u32[]{:S(2)}, u32[]{:S(2)}) collective-permute-start(bf16[2,192,512]{2,1,0:T(8,128)(2,1)S(1)} %get-tuple-element.83.refs_6_), channel_id=1, source_target_pairs={{0,3},{1,0},{2,1},{3,2},{4,7},{5,4},{6,5},{7,6},{8,11},{9,8},{10,9... | collective-permute-start | bytes 1179656 | tf_op jit(solution)/shard_map/ppermute | solution.py:581
  98.2 18.2 %collective-permute-start.12 = (bf16[2,192,512]{2,1,0:T(8,128)(2,1)S(1)}, bf16[2,192,512]{2,1,0:T(8,128)(2,1)S(1)}, u32[]{:S(2)}, u32[]{:S(2)}) collective-permute-start(bf16[2,192,512]{2,1,0:T(8,128)(2,1)S(1)} %get-tuple-element.85), channel_id=1, source_target_pairs={{0,1},{1,2},{2,3},{3,0},{4,5},{5,6},{6,7},{7,4},{8,9},{9,10},{10,1... | collective-permute-start | bytes 1179656 | tf_op jit(solution)/shard_map/ppermute | solution.py:581
  100.1 18.2 %collective-permute-start.16 = (bf16[256,1024]{1,0:T(8,128)(2,1)S(1)}, bf16[256,1024]{1,0:T(8,128)(2,1)S(1)}, u32[]{:S(2)}, u32[]{:S(2)}) collective-permute-start(bf16[256,1024]{1,0:T(8,128)(2,1)S(1)} %get-tuple-element.87), channel_id=1, source_target_pairs={{0,16},{16,0},{1,17},{17,1},{2,18},{18,2},{3,19},{19,3},{4,20},{20... | collective-permute-start | bytes 1572872 | tf_op jit(solution)/shard_map/ppermute | solution.py:595
  101.7 16.7 %collective-permute-start.17 = (bf16[256,1024]{1,0:T(8,128)(2,1)S(1)}, bf16[256,1024]{1,0:T(8,128)(2,1)S(1)}, u32[]{:S(2)}, u32[]{:S(2)}) collective-permute-start(bf16[256,1024]{1,0:T(8,128)(2,1)S(1)} %get-tuple-element.88), channel_id=1, source_target_pairs={{0,8},{4,12},{8,0},{12,4},{1,9},{5,13},{9,1},{13,5},{2,10},{6,14},... | collective-permute-start | bytes 1572872 | tf_op jit(solution)/shard_map/ppermute | solution.py:595
  120.3 9.2 %collective-permute-start.18 = (bf16[128,1024]{1,0:T(8,128)(2,1)S(1)}, bf16[128,1024]{1,0:T(8,128)(2,1)S(1)}, u32[]{:S(2)}, u32[]{:S(2)}) collective-permute-start(bf16[128,1024]{1,0:T(8,128)(2,1)S(1)} %get-tuple-element.90), channel_id=1, source_target_pairs={{0,8},{4,12},{8,0},{12,4},{1,9},{5,13},{9,1},{13,5},{2,10},{6,14},... | collective-permute-start | bytes 786440 | tf_op jit(solution)/shard_map/ppermute | solution.py:595
  121.9 9.1 %collective-permute-start.19 = (bf16[128,1024]{1,0:T(8,128)(2,1)S(1)}, bf16[128,1024]{1,0:T(8,128)(2,1)S(1)}, u32[]{:S(2)}, u32[]{:S(2)}) collective-permute-start(bf16[128,1024]{1,0:T(8,128)(2,1)S(1)} %get-tuple-element.91), channel_id=1, source_target_pairs={{0,16},{16,0},{1,17},{17,1},{2,18},{18,2},{3,19},{19,3},{4,20},{20... | collective-permute-start | bytes 786440 | tf_op jit(solution)/shard_map/ppermute | solution.py:595
  123.6 12.4 %collective-permute-start.24 = (bf16[256,512]{1,0:T(8,128)(2,1)S(1)}, bf16[256,512]{1,0:T(8,128)(2,1)S(1)}, u32[]{:S(2)}, u32[]{:S(2)}) collective-permute-start(bf16[256,512]{1,0:T(8,128)(2,1)S(1)} %get-tuple-element.97), channel_id=1, source_target_pairs={{0,16},{16,0},{1,17},{17,1},{2,18},{18,2},{3,19},{19,3},{4,20},{20... | collective-permute-start | bytes 786440 | tf_op jit(solution)/shard_map/ppermute | solution.py:595
  124.2 11.8 %collective-permute-start.25 = (bf16[256,512]{1,0:T(8,128)(2,1)S(1)}, bf16[256,512]{1,0:T(8,128)(2,1)S(1)}, u32[]{:S(2)}, u32[]{:S(2)}) collective-permute-start(bf16[256,512]{1,0:T(8,128)(2,1)S(1)} %get-tuple-element.98), channel_id=1, source_target_pairs={{0,8},{4,12},{8,0},{12,4},{1,9},{5,13},{9,1},{13,5},{2,10},{6,14},... | collective-permute-start | bytes 786440 | tf_op jit(solution)/shard_map/ppermute | solution.py:595
  131.2 13.0 %collective-permute-start.20 = (bf16[32,2048]{1,0:T(8,128)(2,1)S(1)}, bf16[32,2048]{1,0:T(8,128)(2,1)S(1)}, u32[]{:S(2)}, u32[]{:S(2)}) collective-permute-start(bf16[32,2048]{1,0:T(8,128)(2,1)S(1)} %get-tuple-element.93), channel_id=1, source_target_pairs={{0,1},{1,0},{2,3},{3,2},{4,5},{5,4},{6,7},{7,6},{8,9},{9,8},{10,11... | collective-permute-start | bytes 393224 | tf_op jit(solution)/shard_map/ppermute | solution.py:595
  138.1 15.2 %collective-permute-start.21 = (bf16[32,2048]{1,0:T(8,128)(2,1)S(1)}, bf16[32,2048]{1,0:T(8,128)(2,1)S(1)}, u32[]{:S(2)}, u32[]{:S(2)}) collective-permute-start(bf16[32,2048]{1,0:T(8,128)(2,1)S(1)} %get-tuple-element.94), channel_id=1, source_target_pairs={{0,2},{1,3},{2,0},{3,1},{4,6},{5,7},{6,4},{7,5},{8,10},{9,11},{10,... | collective-permute-start | bytes 393224 | tf_op jit(solution)/shard_map/ppermute | solution.py:595
  139.6 13.6 %collective-permute-start.22 = (bf16[32,2048]{1,0:T(8,128)(2,1)S(1)}, bf16[32,2048]{1,0:T(8,128)(2,1)S(1)}, u32[]{:S(2)}, u32[]{:S(2)}) collective-permute-start(bf16[32,2048]{1,0:T(8,128)(2,1)S(1)} %get-tuple-element.95), channel_id=1, source_target_pairs={{0,3},{1,2},{2,1},{3,0},{4,7},{5,6},{6,5},{7,4},{8,11},{9,10},{10,... | collective-permute-start | bytes 393224 | tf_op jit(solution)/shard_map/ppermute | solution.py:595
  142.3 11.0 %collective-permute-start.28 = (bf16[32,1024]{1,0:T(8,128)(2,1)S(1)}, bf16[32,1024]{1,0:T(8,128)(2,1)S(1)}, u32[]{:S(2)}, u32[]{:S(2)}) collective-permute-start(bf16[32,1024]{1,0:T(8,128)(2,1)S(1)} %get-tuple-element.103), channel_id=1, source_target_pairs={{0,1},{1,0},{2,3},{3,2},{4,5},{5,4},{6,7},{7,6},{8,9},{9,8},{10,11... | collective-permute-start | bytes 196616 | tf_op jit(solution)/shard_map/ppermute | solution.py:595
  143.4 13.4 %collective-permute-start.29 = (bf16[32,1024]{1,0:T(8,128)(2,1)S(1)}, bf16[32,1024]{1,0:T(8,128)(2,1)S(1)}, u32[]{:S(2)}, u32[]{:S(2)}) collective-permute-start(bf16[32,1024]{1,0:T(8,128)(2,1)S(1)} %get-tuple-element.104), channel_id=1, source_target_pairs={{0,2},{1,3},{2,0},{3,1},{4,6},{5,7},{6,4},{7,5},{8,10},{9,11},{10,... | collective-permute-start | bytes 196616 | tf_op jit(solution)/shard_map/ppermute | solution.py:595
  144.1 12.7 %collective-permute-start.30 = (bf16[32,1024]{1,0:T(8,128)(2,1)S(1)}, bf16[32,1024]{1,0:T(8,128)(2,1)S(1)}, u32[]{:S(2)}, u32[]{:S(2)}) collective-permute-start(bf16[32,1024]{1,0:T(8,128)(2,1)S(1)} %get-tuple-element.105), channel_id=1, source_target_pairs={{0,3},{1,2},{2,1},{3,0},{4,7},{5,6},{6,5},{7,4},{8,11},{9,10},{10,... | collective-permute-start | bytes 196616 | tf_op jit(solution)/shard_map/ppermute | solution.py:595
  (20 other events, 183.7 us)
